TPU v7x, 32 devices: a whole 2x2x4 slice. The times are simulated.
32 devices in a mesh: dp: 8 (over z, x), tensor: 4 (over y, core).
Axes of the slice: x: 2, y: 2, z: 4, core: 2. Of those that a mesh axis runs over, the one named last changes fastest.
Arguments:
- hidden: bfloat16 [1024, 4096], P('dp', 'tensor'), may hold values from -6 to 6
- grad_out: bfloat16 [1024, 4096], P('dp', 'tensor'), may hold values from -0.59765625 to 0.59765625
- query_weight: bfloat16 [4096, 4096], P(None, 'tensor'), may hold values from -0.09375 to 0.09375
- key_weight: bfloat16 [768, 4096], P(None, 'tensor'), may hold values from -0.21875 to 0.21875
- value_weight: bfloat16 [768, 4096], P(None, 'tensor'), may hold values from -0.21875 to 0.21875
- out_weight: bfloat16 [4096, 4096], P('tensor', 'dp'), may hold values from -0.75 to 0.75
- neighbour_states: bfloat16 [32, 128, 768], P('dp', None, 'tensor'), may hold values from -6 to 6
- block_owner: int32 [8, 4], P('dp'), may hold values from 0 to 7, as said below
- slot_target: int32 [8, 4], P('dp'), may hold values from 0 to 7, as said below
Outputs:
- cross_out: bfloat16 [1024, 4096], P('dp', 'tensor')
- grad_hidden: bfloat16 [1024, 4096], P('dp', 'tensor')
- grad_states: bfloat16 [32, 128, 768], P('dp', None, 'tensor')
Inputs may be any that keep to these rules, and one draw needn't show every extreme that they name: block_owner[d, t] = o exactly when slot_target[o, t] = d. The blocks 2k and 2k+1 of a dp index share their holder; the difference (holder - d) modulo the dp count is the same for every d, lies in 1 to 4, and differs between k. So a dp index holds exactly 2 blocks for each of 2 other indices. `slot_target`: the inverse map of block_owner, as stated there.
All inputs are finite; a program needn't handle non-finite values.
Results may differ from a plain program's by a relative error of at most 0.012.
Values may be sent and summed in bfloat16 or wider, within the bound.
A program may use at most 128 MiB of HBM per device.

v0:
```python
import math

import jax
import jax.numpy as jnp
from jax import lax
from jax.sharding import PartitionSpec as P

HEADS = 32
SPAN = 64
K_NB = 2
CAP = 2
WINDOW = 4


def shifted(x, axis, by):
    devices = lax.axis_size(axis)
    return lax.ppermute(x, axis, [(i, (i + by) % devices) for i in range(devices)])


def contract_last(left, right):
    return lax.dot_general(
        left, right, (((1,), (1,)), ((), ())), preferred_element_type=jnp.float32
    )


def contract_first(left, right):
    return lax.dot_general(
        left, right, (((0,), (0,)), ((), ())), preferred_element_type=jnp.float32
    )


def shards(
    hidden,
    grad_out,
    query_weight,
    key_weight,
    value_weight,
    out_weight,
    neighbour_states,
    block_owner,
    slot_target,
):
    full_hidden, full_grad = (
        lax.all_gather(hidden, "tensor", axis=1, tiled=True),
        lax.all_gather(grad_out, "tensor", axis=1, tiled=True),
    )
    out_gathered = lax.all_gather(out_weight, "dp", axis=1, tiled=True)
    dp_count = lax.axis_size("dp")
    my_index = lax.axis_index("dp")
    block_count, block_len, width_part = neighbour_states.shape
    block_ids = jnp.arange(block_count, dtype=jnp.int32)
    owner_gap = (block_owner[0] - my_index + dp_count) % dp_count
    target_gap = (my_index - slot_target[0] + dp_count) % dp_count
    pair_ids = jnp.arange(CAP, dtype=jnp.int32)
    flat_states = neighbour_states.reshape(block_count, block_len * width_part)
    delivered = jnp.zeros((block_count, block_len * width_part), jnp.float32)
    for offset in range(1, WINDOW + 1):
        send_table = (
            (target_gap[None, :] == offset) & ((block_ids % CAP)[None, :] == pair_ids[:, None])
        ).astype(jnp.bfloat16)
        receive_table = (
            (owner_gap[:, None] == offset) & ((block_ids % CAP)[:, None] == pair_ids[None, :])
        ).astype(jnp.bfloat16)
        outgoing = jnp.dot(send_table, flat_states, preferred_element_type=jnp.float32).astype(
            jnp.bfloat16
        )
        incoming = shifted(outgoing, "dp", -offset)
        delivered = delivered + jnp.dot(receive_table, incoming, preferred_element_type=jnp.float32)
    delivered = delivered.astype(jnp.bfloat16)
    neighbours = lax.all_gather(
        delivered.reshape(block_count * block_len, width_part), "tensor", axis=1, tiled=True
    )
    query = jnp.dot(full_hidden, query_weight, preferred_element_type=jnp.float32).astype(
        jnp.bfloat16
    )
    key_rows = jnp.dot(neighbours, key_weight, preferred_element_type=jnp.float32).astype(
        jnp.bfloat16
    )
    value_rows = jnp.dot(neighbours, value_weight, preferred_element_type=jnp.float32).astype(
        jnp.bfloat16
    )
    local_heads = HEADS // lax.axis_size("tensor")
    head_size = query.shape[1] // local_heads
    span_count = query.shape[0] // SPAN
    score_scale = 1.0 / math.sqrt(head_size)
    query_heads = query.reshape(span_count, SPAN, local_heads, head_size)
    key_heads = key_rows.reshape(span_count, K_NB * block_len, local_heads, head_size)
    value_heads = value_rows.reshape(span_count, K_NB * block_len, local_heads, head_size)
    scores = (
        jnp.einsum("cqhd,ckhd->chqk", query_heads, key_heads, preferred_element_type=jnp.float32)
        * score_scale
    )
    highest = jnp.max(scores, axis=-1, keepdims=True)
    expanded = jnp.exp(scores - highest)
    probs = expanded / jnp.sum(expanded, axis=-1, keepdims=True)
    probs_low = probs.astype(jnp.bfloat16)
    attended = (
        jnp.einsum("chqk,ckhd->cqhd", probs_low, value_heads, preferred_element_type=jnp.float32)
        .astype(jnp.bfloat16)
        .reshape(query.shape)
    )
    out_partial = jnp.dot(attended, out_gathered, preferred_element_type=jnp.float32).astype(
        jnp.bfloat16
    )
    cross_out = (
        lax.psum_scatter(out_partial, "tensor", scatter_dimension=1, tiled=True)
        .astype(jnp.float32)
        .astype(jnp.bfloat16)
    )
    grad_attended = contract_last(full_grad, out_gathered).astype(jnp.bfloat16)
    grad_heads = grad_attended.reshape(query_heads.shape)
    grad_probs = jnp.einsum(
        "cqhd,ckhd->chqk", grad_heads, value_heads, preferred_element_type=jnp.float32
    )
    grad_scores = (
        probs * (grad_probs - jnp.sum(probs * grad_probs, axis=-1, keepdims=True)) * score_scale
    ).astype(jnp.bfloat16)
    grad_query = (
        jnp.einsum("chqk,ckhd->cqhd", grad_scores, key_heads, preferred_element_type=jnp.float32)
        .astype(jnp.bfloat16)
        .reshape(query.shape)
    )
    grad_key = (
        jnp.einsum("chqk,cqhd->ckhd", grad_scores, query_heads, preferred_element_type=jnp.float32)
        .astype(jnp.bfloat16)
        .reshape(key_rows.shape)
    )
    grad_value = (
        jnp.einsum("chqk,cqhd->ckhd", probs_low, grad_heads, preferred_element_type=jnp.float32)
        .astype(jnp.bfloat16)
        .reshape(value_rows.shape)
    )
    hidden_partial = contract_last(grad_query, query_weight).astype(jnp.bfloat16)
    states_partial = (
        contract_last(grad_key, key_weight) + contract_last(grad_value, value_weight)
    ).astype(jnp.bfloat16)
    hidden_summed, states_summed = (
        lax.psum_scatter(hidden_partial, "tensor", scatter_dimension=1, tiled=True).astype(
            jnp.float32
        ),
        lax.psum_scatter(states_partial, "tensor", scatter_dimension=1, tiled=True).astype(
            jnp.float32
        ),
    )
    grad_hidden = hidden_summed.astype(jnp.bfloat16)
    grad_rows = states_summed.astype(jnp.bfloat16).reshape(block_count, block_len * width_part)
    grad_states = jnp.zeros((block_count, block_len * width_part), jnp.float32)
    for offset in range(1, WINDOW + 1):
        send_table = (
            (target_gap[None, :] == offset) & ((block_ids % CAP)[None, :] == pair_ids[:, None])
        ).astype(jnp.bfloat16)
        receive_table = (
            (owner_gap[:, None] == offset) & ((block_ids % CAP)[:, None] == pair_ids[None, :])
        ).astype(jnp.bfloat16)
        returning = contract_first(receive_table, grad_rows).astype(jnp.bfloat16)
        returned = shifted(returning, "dp", offset)
        grad_states = grad_states + contract_first(send_table, returned)
    grad_states = grad_states.astype(jnp.bfloat16)
    return (cross_out, grad_hidden, grad_states.reshape(block_count, block_len, width_part))


def solution(mesh):
    placed = (
        P("dp", "tensor"),
        P("dp", "tensor"),
        P(None, "tensor"),
        P(None, "tensor"),
        P(None, "tensor"),
        P("tensor", "dp"),
        P("dp", None, "tensor"),
        P("dp", None),
        P("dp", None),
    )
    return jax.shard_map(
        shards,
        mesh=mesh,
        in_specs=placed,
        out_specs=(P("dp", "tensor"), P("dp", "tensor"), P("dp", None, "tensor")),
        check_vma=False,
    )
```

profile of v0, /device:TPU:4, one launch (start us, length us, event | category | flops | bytes accessed | tf_op | source)
XLA Modules:
  0.0 287.9 jit_solution(17136515011482601629)
XLA Ops:
  7.2 0.7 all-gather.4.cloned.1.call-update
  8.0 0.7 all-gather.8.cloned.1.call-update
  8.7 0.7 all-gather.6.cloned.1.call-update
  9.5 1.1 copy.36
  11.1 4.6 %collective-permute-start = (bf16[2,24576]{1,0:T(2,128)(2,1)S(1)}, bf16[2,24576]{1,0:T(2,128)(2,1)S(1)}, u32[]{:S(2)}, u32[]{:S(2)}) collective-permute-start(bf16[2,24576]{1,0:T(2,128)(2,1)S(1)} %convolution_convert_fusion.7), channel_id=1, source_target_pairs={{0,28},{4,0},{8,4},{12,8},{16,12},{20,16},{24,20},{28,24},{1,29},{... | collective-permute-start | bytes 294920 | tf_op jit(solution)/shard_map/ppermute | solution.py:17
  16.0 0.5 collective-permute-start.1
  17.1 3.1 %collective-permute-start.3 = (bf16[2,24576]{1,0:T(2,128)(2,1)S(1)}, bf16[2,24576]{1,0:T(2,128)(2,1)S(1)}, u32[]{:S(2)}, u32[]{:S(2)}) collective-permute-start(bf16[2,24576]{1,0:T(2,128)(2,1)S(1)} %convolution_convert_fusion.4), channel_id=1, source_target_pairs={{0,16},{4,20},{8,24},{12,28},{16,0},{20,4},{24,8},{28,12},{1,17},{... | collective-permute-start | bytes 294920 | tf_op jit(solution)/shard_map/ppermute | solution.py:17
  20.2 8.0 %collective-permute-done.3 = bf16[2,24576]{1,0:T(2,128)(2,1)S(1)} collective-permute-done((bf16[2,24576]{1,0:T(2,128)(2,1)S(1)}, bf16[2,24576]{1,0:T(2,128)(2,1)S(1)}, u32[]{:S(2)}, u32[]{:S(2)}) %collective-permute-start.3) | collective-permute-done | bytes 98336 | tf_op jit(solution)/shard_map/ppermute | solution.py:17
  28.2 0.3 fusion.61
  28.5 0.3 fusion.58
  28.9 0.3 fusion.55
  29.2 0.4 fusion.6
  30.0 7.9 %all_gather.12 = bf16[512,768]{0,1:T(8,128)(2,1)S(1)} all-gather(bf16[512,192]{0,1:T(8,128)(2,1)S(1)} %copy.37), channel_id=1, replica_groups=mesh['dp'=8,'tensor'=4] {'tensor'}, dimensions={1}, use_global_device_ids=true | all-gather | bytes 983040 | tf_op jit(solution)/shard_map/all_gather | solution.py:70
  37.9 1.0 fusion.10
  39.3 1.0 fusion.9
  40.3 1.2 copy.54
  41.5 5.0 %fusion.18 = bf16[16,8,8,128]{3,1,2,0:T(8,128)(2,1)S(1)} fusion(bf16[128,4096]{1,0:T(8,128)(2,1)} %all-gather.4.cloned.1.call-done, bf16[4096,1024]{1,0:T(8,128)(2,1)} %param.11), kind=kOutput, calls=%fused_computation.40 | convolution fusion | flops 1073872896 | bytes 9699328 | tf_op jit(solution)/shard_map/dot_general | solution.py:73
  46.6 0.5 convolution_multiply_fusion
  47.1 1.0 copy-done.2
  48.1 1.3 fusion.112
  49.3 124.0 %all-gather.6.cloned.1.call-done = bf16[1024,4096]{1,0:T(8,128)(2,1)} async-done(((bf16[1024,512]{1,0:T(8,128)(2,1)}), bf16[1024,4096]{1,0:T(8,128)(2,1)}) %all-gather.6.cloned.1.call-update) | async-done | bytes 8388624 | tf_op jit(solution)/shard_map/all_gather | solution.py:47
  173.4 6.7 %fusion.19 = bf16[16,8,8,128]{3,1,2,0:T(8,128)(2,1)S(1)} fusion(bf16[128,4096]{1,0:T(8,128)(2,1)} %all-gather.8.cloned.1.call-done, bf16[1024,4096]{1,0:T(8,128)(2,1)} %all-gather.6.cloned.1.call-done), kind=kOutput, calls=%fused_computation.41 | convolution fusion | flops 1073872896 | bytes 9699328 | tf_op jit(solution)/shard_map/dot_general | solution.py:21
  180.1 1.5 fusion.31
  181.6 4.7 %fusion.12 = bf16[2,256,8,128]{1,3,2,0:T(8,128)(2,1)} fusion(bf16[2,64,8,128]{3,2,1,0:T(8,128)(2,1)S(1)} %bitcast.94, f32[2,8,64]{2,1,0:T(8,128)S(1)} %get-tuple-element.22, f32[2,8,64,256]{3,2,1,0:T(8,128)} %copy-done.2), kind=kOutput, calls=%fused_computation.29 | convolution fusion | flops 68420864 | bytes 2363392 | tf_op jit(solution)/shard_map/chqk,cqhd->ckhd/dot_general | solution.py:129
  186.3 9.0 %fusion.11 = bf16[2,256,8,128]{1,3,2,0:T(8,128)(2,1)} fusion(f32[2,8,64,256]{3,2,1,0:T(8,128)} %fusion.31, bf16[2,64,8,128]{3,2,1,0:T(8,128)(2,1)S(1)} %bitcast.92, f32[2,8,64,256]{3,2,1,0:T(8,128)} %get-tuple-element.23, f32[2,8,64]{2,1,0:T(8,128)S(1)} %get-tuple-element.22), kind=kOutput, calls=%fused_computation.28 | convolution fusion | flops 69469440 | bytes 3411968 | tf_op jit(solution)/shard_map/chqk,cqhd->ckhd/dot_general | solution.py:124
  195.3 2.4 copy.47
  197.8 2.5 copy.49
  200.2 2.4 fusion.24
  202.6 2.0 add_convert_fusion
  204.9 3.7 %fusion.20 = bf16[2,64,8,128]{3,1,2,0:T(8,128)(2,1)S(1)} fusion(bf16[2,256,8,128]{3,2,1,0:T(8,128)(2,1)} %bitcast.88, f32[2,8,64]{2,1,0:T(8,128)S(1)} %get-tuple-element.22, f32[2,8,64,256]{3,2,1,0:T(8,128)} %copy-done.2), kind=kOutput, calls=%fused_computation.42 | convolution fusion | flops 68027648 | bytes 2363392 | tf_op jit(solution)/shard_map/chqk,ckhd->cqhd/dot_general | solution.py:98
  208.8 5.9 %convolution_convert_fusion.9 = bf16[128,4096]{1,0:T(8,128)(2,1)} fusion(bf16[1024,4096]{1,0:T(8,128)(2,1)} %all-gather.6.cloned.1.call-done, bf16[16,8,8,128]{3,2,1,0:T(8,128)(2,1)S(1)} %bitcast.90), kind=kOutput, calls=%fused_computation.19 | convolution fusion | flops 1074266112 | bytes 9699328 | tf_op jit(solution)/shard_map/dot_general | solution.py:102
  214.8 7.7 %fusion.21 = bf16[2,64,8,128]{3,1,2,0:T(8,128)(2,1)S(1)} fusion(f32[2,8,64,256]{3,2,1,0:T(8,128)} %fusion.31, bf16[2,256,8,128]{3,2,1,0:T(8,128)(2,1)S(1)} %bitcast.87, f32[2,8,64,256]{3,2,1,0:T(8,128)} %get-tuple-element.23, f32[2,8,64]{2,1,0:T(8,128)S(1)} %get-tuple-element.22), kind=kOutput, calls=%fused_computation.43 | convolution fusion | flops 69076224 | bytes 3411968 | tf_op jit(solution)/shard_map/chqk,ckhd->cqhd/dot_general | solution.py:119
  222.7 7.3 %convolution_convert_fusion.8 = bf16[128,4096]{1,0:T(8,128)(2,1)} fusion(bf16[4096,1024]{1,0:T(8,128)(2,1)} %param.11, bf16[16,8,8,128]{3,2,1,0:T(8,128)(2,1)S(1)} %bitcast.95), kind=kOutput, calls=%fused_computation.18 | convolution fusion | flops 1074266112 | bytes 9699328 | tf_op jit(solution)/shard_map/dot_general | solution.py:21
  230.0 1.1 copy.50
  231.4 0.4 convolution_convert_fusion
  231.8 1.6 collective-permute-start.7
  233.4 0.4 convolution_convert_fusion.1
  233.7 0.4 convolution_convert_fusion.2
  234.1 0.4 convolution_convert_fusion.3
  234.5 0.5 collective-permute-start.4
  235.0 0.4 collective-permute-start.5
  235.4 2.0 collective-permute-start.6
  237.5 0.8 collective-permute-done.7
  238.5 8.8 %collective-permute-done.6 = bf16[2,24576]{1,0:T(2,128)(2,1)S(1)} collective-permute-done((bf16[2,24576]{1,0:T(2,128)(2,1)S(1)}, bf16[2,24576]{1,0:T(2,128)(2,1)S(1)}, u32[]{:S(2)}, u32[]{:S(2)}) %collective-permute-start.6) | collective-permute-done | bytes 98336 | tf_op jit(solution)/shard_map/ppermute | solution.py:17
  248.0 0.3 fusion.7
  248.6 0.8 copy.51
  249.4 3.8 %reduce-scatter.4.cloned.1.call-done = bf16[128,1024]{1,0:T(8,128)(2,1)} async-done(((bf16[128,4096]{1,0:T(8,128)(2,1)}), bf16[128,1024]{1,0:T(8,128)(2,1)}) %reduce-scatter.4.cloned.1.call-update) | async-done | bytes 262160 | tf_op jit(solution)/shard_map/reduce_scatter | solution.py:106
  253.2 27.9 %reduce-scatter.6.cloned.1.call-done = bf16[128,1024]{1,0:T(8,128)(2,1)} async-done(((bf16[128,4096]{1,0:T(8,128)(2,1)}), bf16[128,1024]{1,0:T(8,128)(2,1)}) %reduce-scatter.6.cloned.1.call-update) | async-done | bytes 262160 | tf_op jit(solution)/shard_map/reduce_scatter | solution.py:138
  (55 shorter events, 4.7 us)
Async XLA Ops:
  7.2 30.7 %copy-start = (bf16[768,1024]{1,0:T(8,128)(2,1)S(1)}, bf16[768,1024]{1,0:T(8,128)(2,1)}, u32[]{:S(2)}) copy-start(bf16[768,1024]{1,0:T(8,128)(2,1)} %param.12) | copy-start | bytes 4718596
  7.2 3.7 %copy-start.4 = (s32[1,4]{1,0:T(1,128)S(1)}, s32[1,4]{1,0:T(1,128)}, u32[]{:S(2)}) copy-start(s32[1,4]{1,0:T(1,128)} %param.17) | copy-start | bytes 52
  7.2 13.0 %copy-start.5 = (s32[1,4]{1,0:T(1,128)S(1)}, s32[1,4]{1,0:T(1,128)}, u32[]{:S(2)}) copy-start(s32[1,4]{1,0:T(1,128)} %param.16) | copy-start | bytes 52
  7.2 34.3 %all-gather.4.cloned.1.call-start = ((), (), s32[]{:S(2)}) async-start(), calls=%async_computation.3 | async-start | bytes 1310720 | tf_op jit(solution)/shard_map/all_gather | solution.py:44
  7.9 41.4 %all-gather.8.cloned.1.call-start = ((), (), s32[]{:S(2)}) async-start(), calls=%async_computation.6 | async-start | bytes 1310720 | tf_op jit(solution)/shard_map/all_gather | solution.py:45
  8.7 164.7 %all-gather.6.cloned.1.call-start = ((), (), s32[]{:S(2)}) async-start(), calls=%async_computation.4 | async-start | bytes 9437184 | tf_op jit(solution)/shard_map/all_gather | solution.py:47
  9.4 220.6 %reduce-scatter.8.cloned.1.call-start = ((), (), s32[]{:S(2)}) async-start(), calls=%async_computation.8 | async-start | bytes 983040 | tf_op jit(solution)/shard_map/reduce_scatter | solution.py:141
  11.1 18.1 %collective-permute-start = (bf16[2,24576]{1,0:T(2,128)(2,1)S(1)}, bf16[2,24576]{1,0:T(2,128)(2,1)S(1)}, u32[]{:S(2)}, u32[]{:S(2)}) collective-permute-start(bf16[2,24576]{1,0:T(2,128)(2,1)S(1)} %convolution_convert_fusion.7), channel_id=1, source_target_pairs={{0,28},{4,0},{8,4},{12,8},{16,12},{20,16},{24,20},{28,24},{1,29},{... | collective-permute-start | bytes 294920 | tf_op jit(solution)/shard_map/ppermute | solution.py:17
  16.0 12.9 %collective-permute-start.1 = (bf16[2,24576]{1,0:T(2,128)(2,1)S(1)}, bf16[2,24576]{1,0:T(2,128)(2,1)S(1)}, u32[]{:S(2)}, u32[]{:S(2)}) collective-permute-start(bf16[2,24576]{1,0:T(2,128)(2,1)S(1)} %convolution_convert_fusion.6), channel_id=1, source_target_pairs={{0,24},{4,28},{8,0},{12,4},{16,8},{20,12},{24,16},{28,20},{1,25},{... | collective-permute-start | bytes 294920 | tf_op jit(solution)/shard_map/ppermute | solution.py:17
  16.7 11.8 %collective-permute-start.2 = (bf16[2,24576]{1,0:T(2,128)(2,1)S(1)}, bf16[2,24576]{1,0:T(2,128)(2,1)S(1)}, u32[]{:S(2)}, u32[]{:S(2)}) collective-permute-start(bf16[2,24576]{1,0:T(2,128)(2,1)S(1)} %convolution_convert_fusion.5), channel_id=1, source_target_pairs={{0,20},{4,24},{8,28},{12,0},{16,4},{20,8},{24,12},{28,16},{1,21},{... | collective-permute-start | bytes 294920 | tf_op jit(solution)/shard_map/ppermute | solution.py:17
  17.1 11.1 %collective-permute-start.3 = (bf16[2,24576]{1,0:T(2,128)(2,1)S(1)}, bf16[2,24576]{1,0:T(2,128)(2,1)S(1)}, u32[]{:S(2)}, u32[]{:S(2)}) collective-permute-start(bf16[2,24576]{1,0:T(2,128)(2,1)S(1)} %convolution_convert_fusion.4), channel_id=1, source_target_pairs={{0,16},{4,20},{8,24},{12,28},{16,0},{20,4},{24,8},{28,12},{1,17},{... | collective-permute-start | bytes 294920 | tf_op jit(solution)/shard_map/ppermute | solution.py:17
  37.9 1.4 copy-start.6
  47.1 1.0 copy-start.2
  173.4 6.8 %copy-start.1 = (bf16[64,8,8,128]{3,2,1,0:T(8,128)(2,1)S(1)}, bf16[64,8,8,128]{3,2,1,0:T(8,128)(2,1)}, u32[]{:S(2)}) copy-start(bf16[64,8,8,128]{3,2,1,0:T(8,128)(2,1)} %copy.54) | copy-start | bytes 3145732
  200.2 2.4 copy-start.3
  200.2 2.4 copy-start.7
  204.6 48.6 %reduce-scatter.4.cloned.1.call-start = ((), (), s32[]{:S(2)}) async-start(), calls=%async_computation.5 | async-start | bytes 1310720 | tf_op jit(solution)/shard_map/reduce_scatter | solution.py:106
  214.7 66.4 %reduce-scatter.6.cloned.1.call-start = ((), (), s32[]{:S(2)}) async-start(), calls=%async_computation.7 | async-start | bytes 1310720 | tf_op jit(solution)/shard_map/reduce_scatter | solution.py:138
  231.8 6.5 %collective-permute-start.7 = (bf16[2,24576]{1,0:T(2,128)(2,1)S(1)}, bf16[2,24576]{1,0:T(2,128)(2,1)S(1)}, u32[]{:S(2)}, u32[]{:S(2)}) collective-permute-start(bf16[2,24576]{1,0:T(2,128)(2,1)S(1)} %convolution_convert_fusion), channel_id=1, source_target_pairs={{0,16},{4,20},{8,24},{12,28},{16,0},{20,4},{24,8},{28,12},{1,17},{... | collective-permute-start | bytes 294920 | tf_op jit(solution)/shard_map/ppermute | solution.py:17
  234.5 13.5 %collective-permute-start.4 = (bf16[2,24576]{1,0:T(2,128)(2,1)S(1)}, bf16[2,24576]{1,0:T(2,128)(2,1)S(1)}, u32[]{:S(2)}, u32[]{:S(2)}) collective-permute-start(bf16[2,24576]{1,0:T(2,128)(2,1)S(1)} %convolution_convert_fusion.3), channel_id=1, source_target_pairs={{0,4},{4,8},{8,12},{12,16},{16,20},{20,24},{24,28},{28,0},{1,5},{5... | collective-permute-start | bytes 294920 | tf_op jit(solution)/shard_map/ppermute | solution.py:17
  235.0 12.6 %collective-permute-start.5 = (bf16[2,24576]{1,0:T(2,128)(2,1)S(1)}, bf16[2,24576]{1,0:T(2,128)(2,1)S(1)}, u32[]{:S(2)}, u32[]{:S(2)}) collective-permute-start(bf16[2,24576]{1,0:T(2,128)(2,1)S(1)} %convolution_convert_fusion.2), channel_id=1, source_target_pairs={{0,8},{4,12},{8,16},{12,20},{16,24},{20,28},{24,0},{28,4},{1,9},{5... | collective-permute-start | bytes 294920 | tf_op jit(solution)/shard_map/ppermute | solution.py:17
  235.4 11.9 %collective-permute-start.6 = (bf16[2,24576]{1,0:T(2,128)(2,1)S(1)}, bf16[2,24576]{1,0:T(2,128)(2,1)S(1)}, u32[]{:S(2)}, u32[]{:S(2)}) collective-permute-start(bf16[2,24576]{1,0:T(2,128)(2,1)S(1)} %convolution_convert_fusion.1), channel_id=1, source_target_pairs={{0,12},{4,16},{8,20},{12,24},{16,28},{20,0},{24,4},{28,8},{1,13},{... | collective-permute-start | bytes 294920 | tf_op jit(solution)/shard_map/ppermute | solution.py:17
Sparse Core Ops, SparseCore 0:
  9.6 16.7 all-gather.3
  28.0 16.7 all-gather.7
  46.8 126.5 all-gather.5
  204.8 20.3 reduce-scatter.7
  228.2 24.9 reduce-scatter.3
  256.2 24.8 reduce-scatter.5
where the time goes:
time: 291 us; the launch traced here: 288 us
  waiting for transfers between devices  175 us (60%)
  matrix products  63.4 us (22%)
  between operations  14.5 us (5%)
  starting transfers between devices  13.2 us (5%)
  local copies, waits for them, and re-layouts  12.2 us (4%)
  blocking collectives  7.88 us (3%)
    all_gather x1, waiting for transfers between devices, shards(): out_gathered = lax.all_gather(out_weight, 'dp', axis=1, tiled=True)  124 us
    reduce_scatter x1, waiting for transfers between devices, shards(): lax.psum_scatter(hidden_partial, 'tensor', scatter_dimension=1, tiled=True)  27.9 us
    dot_general x4, matrix products, contract_last(): lax.dot_general(left, right, (((1,), (1,)), ((), ())), preferred_element_...  18.3 us
    ppermute x8, waiting for transfers between devices, shifted(): lax.ppermute(x, axis, [(i, (i + by) % devices) for i in range(devices)])  17.6 us
    ppermute x8, starting transfers between devices, shifted(): lax.ppermute(x, axis, [(i, (i + by) % devices) for i in range(devices)])  12.8 us
    dot_general x1, matrix products, shards(): jnp.einsum('chqk,cqhd->ckhd', grad_scores, query_heads, preferred_element...  9.03 us
    all_gather x1, blocking collectives, shards(): lax.all_gather(delivered.reshape(block_count * block_len, width_part), 't...  7.88 us
    dot_general x1, matrix products, shards(): jnp.einsum('chqk,ckhd->cqhd', grad_scores, key_heads, preferred_element_t...  7.71 us
  transfers between devices with their start and end apart: 14, of which 6 were waited for; matrix products, arithmetic and copies ran while one was open for 15% of the time, Pallas kernels for 0%

commit v1 on v0

v1 whole, which is shorter than its diff:
```python
import functools
import math

import jax
import jax.numpy as jnp
from jax import lax
from jax.experimental import pallas as pl
from jax.experimental.pallas import tpu as pltpu
from jax.sharding import PartitionSpec as P

HEADS = 32
SPAN = 64
K_NB = 2
CAP = 2
WINDOW = 4
BF = jnp.bfloat16
F32 = jnp.float32


def dot_nt(left, right):
    return lax.dot_general(left, right, (((1,), (1,)), ((), ())), preferred_element_type=F32)


def dot_tn(left, right):
    return lax.dot_general(left, right, (((0,), (0,)), ((), ())), preferred_element_type=F32)


def dot(left, right):
    return jnp.dot(left, right, preferred_element_type=F32)


def softmax_rows(q, k, scale):
    scores = dot_nt(q, k) * scale
    expanded = jnp.exp(scores - jnp.max(scores, axis=-1, keepdims=True))
    return expanded / jnp.sum(expanded, axis=-1, keepdims=True)


def forward_kernel(spans, keys, scale, q_ref, k_ref, v_ref, att_ref):
    for c in range(spans):
        rows, cols = pl.ds(c * SPAN, SPAN), pl.ds(c * keys, keys)
        probs = softmax_rows(q_ref[rows, :], k_ref[cols, :], scale)
        att_ref[rows, :] = dot(probs.astype(BF), v_ref[cols, :]).astype(BF)


def backward_kernel(spans, keys, scale, q_ref, k_ref, v_ref, ga_ref, gq_ref, gk_ref, gv_ref):
    for c in range(spans):
        rows, cols = pl.ds(c * SPAN, SPAN), pl.ds(c * keys, keys)
        q, k, v, ga = q_ref[rows, :], k_ref[cols, :], v_ref[cols, :], ga_ref[rows, :]
        probs = softmax_rows(q, k, scale)
        gp = dot_nt(ga, v)
        gs = (probs * (gp - jnp.sum(probs * gp, axis=-1, keepdims=True)) * scale).astype(BF)
        gq_ref[rows, :] = dot(gs, k).astype(BF)
        gk_ref[cols, :] = dot_tn(gs, q).astype(BF)
        gv_ref[cols, :] = dot_tn(probs.astype(BF), ga).astype(BF)


def per_head(kernel, head_size, arrays, outs):
    heads = arrays[0].shape[1] // head_size

    def block(rows):
        return pl.BlockSpec((rows, head_size), lambda h: (0, h))

    flops = 2 * 6 * arrays[0].shape[0] * 256 * arrays[0].shape[1]
    return pl.pallas_call(
        kernel,
        grid=(heads,),
        in_specs=[block(a.shape[0]) for a in arrays],
        out_specs=[block(a.shape[0]) for a in outs],
        out_shape=[jax.ShapeDtypeStruct(a.shape, BF) for a in outs],
        cost_estimate=pl.CostEstimate(
            flops=flops, bytes_accessed=2 * sum(a.size for a in arrays + outs), transcendentals=0
        ),
        compiler_params=pltpu.CompilerParams(vmem_limit_bytes=32 * 2**20),
    )(*arrays)


def shards(
    hidden,
    grad_out,
    query_weight,
    key_weight,
    value_weight,
    out_weight,
    neighbour_states,
    block_owner,
    slot_target,
):
    dp_count, tp = lax.axis_size("dp"), lax.axis_size("tensor")
    g = dp_count // tp
    d, t = lax.axis_index("dp"), lax.axis_index("tensor")
    zz, gx = d // g, d % g
    tokens, width = hidden.shape
    block_count, block_len, width_part = neighbour_states.shape

    def over_tensor(x, k):
        return lax.ppermute(x, "tensor", [(i, i ^ k) for i in range(tp)])

    def over_zz(x, j):
        return lax.ppermute(x, "dp", [(i, (i // g ^ j) * g + i % g) for i in range(dp_count)])

    def transposed(x):
        pairs = [
            (((a * g + b) * tp + c), ((c * g + b) * tp + a))
            for a in range(tp)
            for b in range(g)
            for c in range(tp)
        ]
        return lax.ppermute(x, ("dp", "tensor"), pairs)

    owner_gap = (block_owner[0] - d + dp_count) % dp_count
    target_gap = (d - slot_target[0] + dp_count) % dp_count
    low, high = neighbour_states[:CAP], neighbour_states[CAP:]
    arrived = []
    for offset in range(1, WINDOW + 1):
        outgoing = jnp.where(target_gap[CAP] == offset, high, low)
        arrived.append(
            lax.ppermute(
                outgoing, "dp", [(i, (i - offset) % dp_count) for i in range(dp_count)]
            )
        )

    turned = transposed(grad_out)
    hidden_parts = [hidden] + [over_tensor(hidden, k) for k in range(1, tp)]
    weight = jnp.zeros((out_weight.shape[0], out_weight.shape[1] * g), BF)
    for k in range(g):
        part = out_weight
        if k:
            part = lax.ppermute(
                part, "dp", [(i, i // g * g + (i - k) % g) for i in range(dp_count)]
            )
        weight = lax.dynamic_update_slice(weight, part, (0, (gx + k) % g * out_weight.shape[1]))

    halves = []
    for k in range(block_count // CAP):
        picked = arrived[0]
        for offset in range(2, WINDOW + 1):
            picked = jnp.where(owner_gap[k * CAP] == offset, arrived[offset - 1], picked)
        halves.append(picked)
    delivered = jnp.concatenate(halves, axis=0).reshape(block_count * block_len, width_part)

    neighbours = jnp.zeros((tp, block_count * block_len, width_part), BF)
    for k in range(tp):
        part = over_tensor(delivered, k) if k else delivered
        neighbours = lax.dynamic_update_slice(neighbours, part[None], (t ^ k, 0, 0))
    neighbours = jnp.concatenate([neighbours[k] for k in range(tp)], axis=1)

    turned_all = jnp.concatenate(
        [turned] + [over_tensor(turned, k) for k in range(1, tp)], axis=0
    )
    partial = dot_nt(turned_all, weight).astype(BF).reshape(tp, tokens, -1)

    def piece(stack, index):
        return lax.dynamic_index_in_dim(stack, index, 0, keepdims=False)

    grad_attended = piece(partial, t ^ zz).astype(F32)
    for j in range(1, tp):
        grad_attended += over_zz(piece(partial, t ^ zz ^ j), j).astype(F32)
    grad_attended = grad_attended.astype(BF)

    query = jnp.zeros((tokens, query_weight.shape[1]), F32)
    for k in range(tp):
        rows = lax.dynamic_slice_in_dim(query_weight, (t ^ k) * width, width, 0)
        query += dot(hidden_parts[k], rows)
    query = query.astype(BF)
    key = dot(neighbours, key_weight).astype(BF)
    value = dot(neighbours, value_weight).astype(BF)

    head_size = query.shape[1] * tp // HEADS
    spans = tokens // SPAN
    scale = 1.0 / math.sqrt(head_size)
    keys = K_NB * block_len
    (attended,) = per_head(
        functools.partial(forward_kernel, spans, keys, scale),
        head_size,
        [query, key, value],
        [query],
    )

    attended_all = jnp.concatenate(
        [attended] + [over_zz(attended, j) for j in range(1, tp)], axis=0
    )
    out_partial = dot(attended_all, weight).astype(BF).reshape(tp, tokens, -1)
    out_sum = piece(out_partial, zz ^ t).astype(F32)
    for k in range(1, tp):
        out_sum += over_tensor(piece(out_partial, zz ^ t ^ k), k).astype(F32)
    cross_out = transposed(out_sum.astype(BF))

    grad_query, grad_key, grad_value = per_head(
        functools.partial(backward_kernel, spans, keys, scale),
        head_size,
        [query, key, value, grad_attended],
        [query, key, value],
    )

    states_partial = (dot_nt(grad_key, key_weight) + dot_nt(grad_value, value_weight)).astype(BF)
    states_partial = jnp.stack(jnp.split(states_partial, tp, axis=1))
    states_sum = piece(states_partial, t).astype(F32)
    for k in range(1, tp):
        states_sum += over_tensor(piece(states_partial, t ^ k), k).astype(F32)
    grad_rows = states_sum.astype(BF).reshape(block_count, block_len, width_part)
    low, high = grad_rows[:CAP], grad_rows[CAP:]
    returned = []
    for offset in range(1, WINDOW + 1):
        outgoing = jnp.where(owner_gap[CAP] == offset, high, low)
        returned.append(
            lax.ppermute(
                outgoing, "dp", [(i, (i + offset) % dp_count) for i in range(dp_count)]
            )
        )
    halves = []
    for k in range(block_count // CAP):
        picked = returned[0]
        for offset in range(2, WINDOW + 1):
            picked = jnp.where(target_gap[k * CAP] == offset, returned[offset - 1], picked)
        halves.append(picked)
    grad_states = jnp.concatenate(halves, axis=0)

    def hidden_piece(k):
        rows = lax.dynamic_slice_in_dim(query_weight, (t ^ k) * width, width, 0)
        return dot_nt(grad_query, rows).astype(BF)

    grad_hidden = hidden_piece(0).astype(F32)
    for k in range(1, tp):
        grad_hidden += over_tensor(hidden_piece(k), k).astype(F32)
    return (cross_out, grad_hidden.astype(BF), grad_states)


def solution(mesh):
    placed = (
        P("dp", "tensor"),
        P("dp", "tensor"),
        P(None, "tensor"),
        P(None, "tensor"),
        P(None, "tensor"),
        P("tensor", "dp"),
        P("dp", None, "tensor"),
        P("dp", None),
        P("dp", None),
    )
    return jax.shard_map(
        shards,
        mesh=mesh,
        in_specs=placed,
        out_specs=(P("dp", "tensor"), P("dp", "tensor"), P("dp", None, "tensor")),
        check_vma=False,
    )
```

time: 291 us -> 174 us (0.60)
  waiting for transfers between devices: 175 us -> 53.5 us
  matrix products: 63.4 us -> 23.9 us
  starting transfers between devices: 13.2 us -> 52.3 us
  Pallas kernels: 0 us -> 17 us
  blocking collectives: 7.88 us -> 0 us
  other arithmetic: 1.32 us -> 6.81 us
  between operations: 14.5 us -> 9.87 us
    all_gather x3 -> x0, waiting for transfers between devices: 124 us -> none  [the longest x1 124 us: shards(): out_gathered = lax.all_gather(out_weight, 'dp', axis=1, tiled=True)]
    ppermute x8 -> x35, starting transfers between devices: 12.8 us -> 52.3 us  [the longest x18 18.9 us: over_tensor(): return lax.ppermute(x, 'tensor', [(i, i ^ k) for i in range(tp)])]
    dot_general x30 -> x14, matrix products: 63.4 us -> 23.9 us  [the longest x7 13.4 us: dot(): return jnp.dot(left, right, preferred_element_type=F32)]
    ppermute x8 -> x35, waiting for transfers between devices: 17.6 us -> 53.5 us  [the longest x18 23.8 us: over_tensor(): return lax.ppermute(x, 'tensor', [(i, i ^ k) for i in range(tp)])]
    reduce_scatter x3 -> x0, waiting for transfers between devices: 31.7 us -> none  [the longest x1 27.9 us: shards(): lax.psum_scatter(hidden_partial, 'tensor', scatter_dimension=1, tiled=True)]
    pallas_call x0 -> x2, Pallas kernels: none -> 17 us  [per_head(): pl.pallas_call(kernel, grid=(heads,), in_specs=[block(a.shape[0]) for a i...]
    all_gather x1 -> x0, blocking collectives: 7.88 us -> none  [shards(): lax.all_gather(delivered.reshape(block_count * block_len, width_part), 't...]
    convert_element_type x4 -> x0, local copies, waits for them, and re-layouts: 5.23 us -> none  [the longest x1 2.45 us: shards(): grad_value = jnp.einsum('chqk,cqhd->ckhd', probs_low, grad_heads, preferr...]
  transfers between devices with their start and end apart: 14 -> 35, of which waited for: 6 -> 11; matrix products, arithmetic and copies ran while one was open for 15% -> 22% of each run, Pallas kernels for 0% -> 10%
where the time goes in v1:
time: 174 us; the launch traced here: 173 us
  waiting for transfers between devices  53.5 us (31%)
  starting transfers between devices  52.3 us (30%)
  matrix products  23.9 us (14%)
  Pallas kernels  17 us (10%)
  between operations  9.87 us (6%)
  local copies, waits for them, and re-layouts  9.43 us (5%)
  other arithmetic  6.81 us (4%)
    ppermute x18, waiting for transfers between devices, over_tensor(): return lax.ppermute(x, 'tensor', [(i, i ^ k) for i in range(tp)])  23.8 us
    ppermute x6, waiting for transfers between devices, over_zz(): lax.ppermute(x, 'dp', [(i, (i // g ^ j) * g + i % g) for i in range(dp_co...  20.8 us
    ppermute x18, starting transfers between devices, over_tensor(): return lax.ppermute(x, 'tensor', [(i, i ^ k) for i in range(tp)])  18.9 us
    pallas_call x2, Pallas kernels, per_head(): pl.pallas_call(kernel, grid=(heads,), in_specs=[block(a.shape[0]) for a i...  17 us
    ppermute x6, starting transfers between devices, over_zz(): lax.ppermute(x, 'dp', [(i, (i // g ^ j) * g + i % g) for i in range(dp_co...  15.1 us
    dot_general x7, matrix products, dot(): return jnp.dot(left, right, preferred_element_type=F32)  13.4 us
    dot_general x7, matrix products, dot_nt(): lax.dot_general(left, right, (((1,), (1,)), ((), ())), preferred_element_...  10.5 us
    ppermute x4, waiting for transfers between devices, shards(): lax.ppermute(outgoing, 'dp', [(i, (i + offset) % dp_count) for i in range...  8.18 us
  transfers between devices with their start and end apart: 35, of which 11 were waited for; matrix products, arithmetic and copies ran while one was open for 22% of the time, Pallas kernels for 10%

profile of v1, /device:TPU:4, one launch (start us, length us, event | category | flops | bytes accessed | tf_op | source)
XLA Modules:
  0.0 172.8 jit_solution(18130446504707468898)
XLA Ops:
  0.6 1.6 collective-permute-start.13
  6.1 1.7 broadcast_select_fusion.4
  7.8 2.6 %collective-permute-start.3 = (bf16[2,128,192]{1,2,0:T(8,128)(2,1)}, bf16[2,128,192]{1,2,0:T(8,128)(2,1)S(1)}, u32[]{:S(2)}, u32[]{:S(2)}) collective-permute-start(bf16[2,128,192]{1,2,0:T(8,128)(2,1)} %get-tuple-element.38), channel_id=1, source_target_pairs={{0,16},{4,20},{8,24},{12,28},{16,0},{20,4},{24,8},{28,12},{1,17},{... | collective-permute-start | bytes 294920 | tf_op jit(solution)/shard_map/ppermute | solution.py:117
  10.7 3.6 %collective-permute-start.5 = (bf16[2,128,192]{1,2,0:T(8,128)(2,1)}, bf16[2,128,192]{1,2,0:T(8,128)(2,1)}, u32[]{:S(2)}, u32[]{:S(2)}) collective-permute-start(bf16[2,128,192]{1,2,0:T(8,128)(2,1)} %get-tuple-element.37), channel_id=1, source_target_pairs={{0,24},{4,28},{8,0},{12,4},{16,8},{20,12},{24,16},{28,20},{1,25},{... | collective-permute-start | bytes 294920 | tf_op jit(solution)/shard_map/ppermute | solution.py:117
  14.3 1.5 collective-permute-start.6
  22.6 2.2 %fusion.14 = f32[1024,128]{0,1:T(8,128)S(1)} fusion(bf16[128,1024]{1,0:T(8,128)(2,1)} %param.9, bf16[4096,1024]{1,0:T(8,128)(2,1)} %param.11, s32[]{:T(128)S(6)} %select_n.213), kind=kOutput, calls=%fused_computation.14 | convolution fusion | flops 268435456 | bytes 2883588 | tf_op jit(solution)/shard_map/dot_general | solution.py:29
  24.8 1.6 broadcast_in_dim.19
  26.5 1.1 constant_dynamic-update-slice_fusion.1
  28.2 1.3 collective-permute-start
  30.1 4.4 %collective-permute-start.18 = (bf16[128,1024]{1,0:T(8,128)(2,1)}, bf16[128,1024]{1,0:T(8,128)(2,1)}, u32[]{:S(2)}, u32[]{:S(2)}) collective-permute-start(bf16[128,1024]{1,0:T(8,128)(2,1)} %param.10), channel_id=1, source_target_pairs={{0,0},{1,8},{2,16},{3,24},{4,4},{5,12},{6,20},{7,28},{8,1},{9,9},{... | collective-permute-start | bytes 786440 | tf_op jit(solution)/shard_map/ppermute | solution.py:108
  34.6 1.0 select_select_fusion.3
  37.2 2.1 %fusion.2 = f32[1024,128]{0,1:T(8,128)S(1)} fusion(bf16[128,1024]{1,0:T(8,128)(2,1)} %collective-permute-done.2, bf16[4096,1024]{1,0:T(8,128)(2,1)} %param.11, s32[]{:T(128)S(6)} %select_n.216), kind=kOutput, calls=%fused_computation.2 | convolution fusion | flops 268435456 | bytes 2883588 | tf_op jit(solution)/shard_map/dot_general | solution.py:29
  39.4 4.0 %collective-permute-done.1 = bf16[128,1024]{1,0:T(8,128)(2,1)} collective-permute-done((bf16[128,1024]{1,0:T(8,128)(2,1)S(1)}, bf16[128,1024]{1,0:T(8,128)(2,1)}, u32[]{:S(2)}, u32[]{:S(2)}) %collective-permute-start.1) | collective-permute-done | bytes 262176 | tf_op jit(solution)/shard_map/ppermute | solution.py:96
  43.4 2.1 %fusion.6 = f32[1024,128]{0,1:T(8,128)S(1)} fusion(bf16[128,1024]{1,0:T(8,128)(2,1)} %collective-permute-done.1, bf16[4096,1024]{1,0:T(8,128)(2,1)} %param.11, s32[]{:T(128)S(6)} %select_n.215), kind=kOutput, calls=%fused_computation.6 | convolution fusion | flops 268435456 | bytes 2883588 | tf_op jit(solution)/shard_map/dot_general | solution.py:29
  45.5 3.4 %collective-permute-start.9 = (bf16[512,192]{0,1:T(8,128)(2,1)S(1)}, bf16[512,192]{0,1:T(8,128)(2,1)S(1)}, u32[]{:S(2)}, u32[]{:S(2)}) collective-permute-start(bf16[512,192]{0,1:T(8,128)(2,1)S(1)} %bitcast.110), channel_id=1, source_target_pairs={{0,3},{1,2},{2,1},{3,0},{4,7},{5,6},{6,5},{7,4},{8,11},{9,10},{10,... | collective-permute-start | bytes 589832 | tf_op jit(solution)/shard_map/ppermute | solution.py:96
  49.0 2.1 %fusion.43.q_ref = bf16[128,1024]{1,0:T(8,128)(2,1)S(1)} fusion(f32[1024,128]{0,1:T(8,128)S(1)} %fusion.2, f32[1024,128]{0,1:T(8,128)S(1)} %fusion.6, f32[1024,128]{0,1:T(8,128)S(1)} %fusion.14, bf16[128,1024]{1,0:T(8,128)(2,1)S(1)} %collective-permute-done, bf16[4096,1024]{1,0:T(8,128)(2,1)} %param.11, s32[]{:T(128)S(6)} %select_n.214), kind=kOutput, calls=%fused_computation.30 | convolution fusion | flops 268959744 | bytes 4194308 | tf_op jit(solution)/shard_map/dot_general | solution.py:29
  51.6 1.5 collective-permute-start.19
  53.1 3.3 %collective-permute-done.9 = bf16[512,192]{0,1:T(8,128)(2,1)S(1)} collective-permute-done((bf16[512,192]{0,1:T(8,128)(2,1)S(1)}, bf16[512,192]{0,1:T(8,128)(2,1)S(1)}, u32[]{:S(2)}, u32[]{:S(2)}) %collective-permute-start.9) | collective-permute-done | bytes 196640 | tf_op jit(solution)/shard_map/ppermute | solution.py:96
  56.5 1.0 convolution_convert_fusion.1.k_ref
  57.9 1.0 convolution_convert_fusion.v_ref
  58.9 6.9 %shard_map.112 = bf16[128,1024]{1,0:T(8,128)(2,1)S(1)} custom-call(bf16[128,1024]{1,0:T(8,128)(2,1)S(1)} %fusion.43.q_ref, bf16[512,1024]{1,0:T(8,128)(2,1)S(1)} %convolution_convert_fusion.1.k_ref, bf16[512,1024]{1,0:T(8,128)(2,1)S(1)} %convolution_convert_fusion.v_ref), custom_call_target="tpu_custom_call" | custom-call | flops 402653184 | bytes 2621440 | tf_op jit(solution)/shard_map/pallas_call | solution.py:64
  66.7 2.4 %constant_dynamic-update-slice_fusion = bf16[1024,1024]{1,0:T(8,128)(2,1)} fusion(bf16[1024,1024]{1,0:T(8,128)(2,1)} %constant_dynamic-update-slice_fusion.1, bf16[1024,512]{1,0:T(8,128)(2,1)} %collective-permute-done.13, s32[]{:T(128)S(6)} %select_n.247), kind=kLoop, calls=%fused_computation.99 | loop fusion | bytes 2097156 | tf_op jit(solution)/shard_map/dynamic_update_slice | solution.py:131
  69.0 3.6 %collective-permute-start.10 = (bf16[128,1024]{1,0:T(8,128)(2,1)S(1)}, bf16[128,1024]{1,0:T(8,128)(2,1)S(1)}, u32[]{:S(2)}, u32[]{:S(2)}) collective-permute-start(bf16[128,1024]{1,0:T(8,128)(2,1)S(1)} %shard_map.112), channel_id=1, source_target_pairs={{0,8},{4,12},{8,0},{12,4},{16,24},{20,28},{24,16},{28,20},{1,9},{5... | collective-permute-start | bytes 786440 | tf_op jit(solution)/shard_map/ppermute | solution.py:99
  72.7 3.0 %convolution_convert_fusion.2 = bf16[512,1024]{1,0:T(8,128)(2,1)S(1)} fusion(bf16[1024,1024]{1,0:T(8,128)(2,1)} %constant_dynamic-update-slice_fusion, bf16[128,1024]{1,0:T(8,128)(2,1)S(1)} %collective-permute-done.21, bf16[128,1024]{1,0:T(8,128)(2,1)S(1)} %collective-permute-done.20, bf16[128,1024]{1,0:T(8,128)(2,1)S(1)} %collective-permute-done.19, ...), kind=kOutput, calls=%fused_computation.19 | convolution fusion | flops 1078460416 | bytes 4194304 | tf_op jit(solution)/shard_map/dot_general | solution.py:21
  75.9 1.4 collective-permute-start.23
  77.3 9.1 %collective-permute-start.22 = (bf16[128,1024]{1,0:T(8,128)(2,1)S(1)}, bf16[128,1024]{1,0:T(8,128)(2,1)S(1)}, u32[]{:S(2)}, u32[]{:S(2)}) collective-permute-start(bf16[128,1024]{1,0:T(8,128)(2,1)S(1)} %get-tuple-element.12), channel_id=1, source_target_pairs={{0,8},{4,12},{8,0},{12,4},{16,24},{20,28},{24,16},{28,20},{1,9},{5... | collective-permute-start | bytes 786440 | tf_op jit(solution)/shard_map/ppermute | solution.py:99
  86.4 15.5 %collective-permute-done.11 = bf16[128,1024]{1,0:T(8,128)(2,1)S(1)} collective-permute-done((bf16[128,1024]{1,0:T(8,128)(2,1)S(1)}, bf16[128,1024]{1,0:T(8,128)(2,1)S(1)}, u32[]{:S(2)}, u32[]{:S(2)}) %collective-permute-start.11) | collective-permute-done | bytes 262176 | tf_op jit(solution)/shard_map/ppermute | solution.py:99
  101.9 2.8 %convolution_convert_fusion.3 = bf16[512,1024]{1,0:T(8,128)(2,1)S(1)} fusion(bf16[1024,1024]{1,0:T(8,128)(2,1)} %constant_dynamic-update-slice_fusion, bf16[128,1024]{1,0:T(8,128)(2,1)S(1)} %collective-permute-done.12, bf16[128,1024]{1,0:T(8,128)(2,1)S(1)} %collective-permute-done.11, bf16[128,1024]{1,0:T(8,128)(2,1)S(1)} %collective-permute-done.10, ...), kind=kOutput, calls=%fused_computation.20 | convolution fusion | flops 1078460416 | bytes 4194304 | tf_op jit(solution)/shard_map/dot_general | solution.py:29
  104.8 1.2 collective-permute-start.16
  106.8 5.3 %collective-permute-done.23 = bf16[128,1024]{1,0:T(8,128)(2,1)S(1)} collective-permute-done((bf16[128,1024]{1,0:T(8,128)(2,1)S(1)}, bf16[128,1024]{1,0:T(8,128)(2,1)S(1)}, u32[]{:S(2)}, u32[]{:S(2)}) %collective-permute-start.23) | collective-permute-done | bytes 262176 | tf_op jit(solution)/shard_map/ppermute | solution.py:99
  112.2 10.0 %shard_map.113 = (bf16[128,1024]{1,0:T(8,128)(2,1)S(1)}, bf16[512,1024]{1,0:T(8,128)(2,1)S(1)}, bf16[512,1024]{1,0:T(8,128)(2,1)S(1)}) custom-call(bf16[128,1024]{1,0:T(8,128)(2,1)S(1)} %fusion.43.q_ref, bf16[512,1024]{1,0:T(8,128)(2,1)S(1)} %convolution_convert_fusion.1.k_ref, bf16[512,1024]{1,0:T(8,128)(2,1)S(1)} %convolution_convert_fusion.v_ref, ...), custom_call_target="tpu_custom_call" | custom-call | flops 402653184 | bytes 4980736 | tf_op jit(solution)/shard_map/pallas_call | solution.py:64
  122.3 1.5 fusion.40
  123.8 1.5 fusion.37
  126.4 2.1 %collective-permute-start.17 = (bf16[128,1024]{1,0:T(8,128)(2,1)S(1)}, bf16[128,1024]{1,0:T(8,128)(2,1)S(1)}, u32[]{:S(2)}, u32[]{:S(2)}) collective-permute-start(bf16[128,1024]{1,0:T(8,128)(2,1)S(1)} %fusion.68), channel_id=1, source_target_pairs={{0,0},{1,8},{2,16},{3,24},{4,4},{5,12},{6,20},{7,28},{8,1},{9,9},{... | collective-permute-start | bytes 786440 | tf_op jit(solution)/shard_map/ppermute | solution.py:108
  128.5 0.9 collective-permute-start.27
  129.5 1.0 fusion.86
  130.5 1.0 add_convert_fusion
  132.1 0.9 collective-permute-start.30
  133.0 2.8 %collective-permute-start.29 = (bf16[512,192]{1,0:T(8,128)(2,1)S(1)}, bf16[512,192]{1,0:T(8,128)(2,1)S(1)}, u32[]{:S(2)}, u32[]{:S(2)}) collective-permute-start(bf16[512,192]{1,0:T(8,128)(2,1)S(1)} %get-tuple-element.11), channel_id=1, source_target_pairs={{0,2},{1,3},{2,0},{3,1},{4,6},{5,7},{6,4},{7,5},{8,10},{9,11},{10,... | collective-permute-start | bytes 589832 | tf_op jit(solution)/shard_map/ppermute | solution.py:96
  135.8 1.5 fusion.34
  137.4 9.0 %collective-permute-done.30 = bf16[512,192]{1,0:T(8,128)(2,1)S(1)} collective-permute-done((bf16[512,192]{1,0:T(8,128)(2,1)S(1)}, bf16[512,192]{1,0:T(8,128)(2,1)S(1)}, u32[]{:S(2)}, u32[]{:S(2)}) %collective-permute-start.30) | collective-permute-done | bytes 196640 | tf_op jit(solution)/shard_map/ppermute | solution.py:96
  146.4 4.1 %collective-permute-start.26 = (bf16[128,1024]{1,0:T(8,128)(2,1)}, bf16[128,1024]{1,0:T(8,128)(2,1)}, u32[]{:S(2)}, u32[]{:S(2)}) collective-permute-start(bf16[128,1024]{1,0:T(8,128)(2,1)} %fusion.37), channel_id=1, source_target_pairs={{0,2},{1,3},{2,0},{3,1},{4,6},{5,7},{6,4},{7,5},{8,10},{9,11},{10,... | collective-permute-start | bytes 786440 | tf_op jit(solution)/shard_map/ppermute | solution.py:96
  150.5 4.5 %collective-permute-done.29 = bf16[512,192]{1,0:T(8,128)(2,1)S(1)} collective-permute-done((bf16[512,192]{1,0:T(8,128)(2,1)S(1)}, bf16[512,192]{1,0:T(8,128)(2,1)S(1)}, u32[]{:S(2)}, u32[]{:S(2)}) %collective-permute-start.29) | collective-permute-done | bytes 196640 | tf_op jit(solution)/shard_map/ppermute | solution.py:96
  157.2 2.8 %collective-permute-done.26 = bf16[128,1024]{1,0:T(8,128)(2,1)} collective-permute-done((bf16[128,1024]{1,0:T(8,128)(2,1)}, bf16[128,1024]{1,0:T(8,128)(2,1)}, u32[]{:S(2)}, u32[]{:S(2)}) %collective-permute-start.26) | collective-permute-done | bytes 262176 | tf_op jit(solution)/shard_map/ppermute | solution.py:96
  160.1 1.2 collective-permute-start.34
  161.3 1.9 %add_convert_fusion.1 = bf16[128,1024]{1,0:T(8,128)(2,1)} fusion(bf16[128,1024]{1,0:T(8,128)(2,1)S(1)} %collective-permute-done.27, bf16[128,1024]{1,0:T(8,128)(2,1)} %collective-permute-done.26, f32[128,1024]{1,0:T(8,128)S(1)} %fusion.31, bf16[128,1024]{1,0:T(8,128)(2,1)} %collective-permute-done.25), kind=kLoop, calls=%fused_computation.59 | loop fusion | flops 917504 | bytes 1572864 | tf_op jit(solution)/shard_map/convert_element_type | solution.py:225
  163.1 4.5 %collective-permute-done.31 = bf16[2,128,192]{1,2,0:T(8,128)(2,1)S(1)} collective-permute-done((bf16[2,128,192]{1,2,0:T(8,128)(2,1)S(1)}, bf16[2,128,192]{1,2,0:T(8,128)(2,1)S(1)}, u32[]{:S(2)}, u32[]{:S(2)}) %collective-permute-start.31) | collective-permute-done | bytes 98336 | tf_op jit(solution)/shard_map/ppermute | solution.py:206
  167.7 3.6 %collective-permute-done.32 = bf16[2,128,192]{1,2,0:T(8,128)(2,1)S(1)} collective-permute-done((bf16[2,128,192]{1,2,0:T(8,128)(2,1)}, bf16[2,128,192]{1,2,0:T(8,128)(2,1)S(1)}, u32[]{:S(2)}, u32[]{:S(2)}) %collective-permute-start.32) | collective-permute-done | bytes 98336 | tf_op jit(solution)/shard_map/ppermute | solution.py:206
  (86 shorter events, 13.4 us)
Async XLA Ops:
  0.6 55.8 %copy-start = (bf16[768,1024]{1,0:T(8,128)(2,1)S(1)}, bf16[768,1024]{1,0:T(8,128)(2,1)}, u32[]{:S(2)}) copy-start(bf16[768,1024]{1,0:T(8,128)(2,1)} %param.12) | copy-start | bytes 4718596
  0.6 65.3 %collective-permute-start.13 = (bf16[1024,512]{1,0:T(8,128)(2,1)}, bf16[1024,512]{1,0:T(8,128)(2,1)}, u32[]{:S(2)}, u32[]{:S(2)}) collective-permute-start(bf16[1024,512]{1,0:T(8,128)(2,1)} %param.14), channel_id=1, source_target_pairs={{0,4},{4,0},{8,12},{12,8},{16,20},{20,16},{24,28},{28,24},{1,5},{5... | collective-permute-start | bytes 3145736 | tf_op jit(solution)/shard_map/ppermute | solution.py:128
  7.8 19.8 %collective-permute-start.3 = (bf16[2,128,192]{1,2,0:T(8,128)(2,1)}, bf16[2,128,192]{1,2,0:T(8,128)(2,1)S(1)}, u32[]{:S(2)}, u32[]{:S(2)}) collective-permute-start(bf16[2,128,192]{1,2,0:T(8,128)(2,1)} %get-tuple-element.38), channel_id=1, source_target_pairs={{0,16},{4,20},{8,24},{12,28},{16,0},{20,4},{24,8},{28,12},{1,17},{... | collective-permute-start | bytes 294920 | tf_op jit(solution)/shard_map/ppermute | solution.py:117
  10.4 17.2 %collective-permute-start.4 = (bf16[2,128,192]{1,2,0:T(8,128)(2,1)}, bf16[2,128,192]{1,2,0:T(8,128)(2,1)}, u32[]{:S(2)}, u32[]{:S(2)}) collective-permute-start(bf16[2,128,192]{1,2,0:T(8,128)(2,1)} %get-tuple-element.39), channel_id=1, source_target_pairs={{0,20},{4,24},{8,28},{12,0},{16,4},{20,8},{24,12},{28,16},{1,21},{... | collective-permute-start | bytes 294920 | tf_op jit(solution)/shard_map/ppermute | solution.py:117
  10.7 17.5 %collective-permute-start.5 = (bf16[2,128,192]{1,2,0:T(8,128)(2,1)}, bf16[2,128,192]{1,2,0:T(8,128)(2,1)}, u32[]{:S(2)}, u32[]{:S(2)}) collective-permute-start(bf16[2,128,192]{1,2,0:T(8,128)(2,1)} %get-tuple-element.37), channel_id=1, source_target_pairs={{0,24},{4,28},{8,0},{12,4},{16,8},{20,12},{24,16},{28,20},{1,25},{... | collective-permute-start | bytes 294920 | tf_op jit(solution)/shard_map/ppermute | solution.py:117
  14.3 15.9 %collective-permute-start.6 = (bf16[2,128,192]{1,2,0:T(8,128)(2,1)}, bf16[2,128,192]{1,2,0:T(8,128)(2,1)}, u32[]{:S(2)}, u32[]{:S(2)}) collective-permute-start(bf16[2,128,192]{1,2,0:T(8,128)(2,1)} %get-tuple-element.36), channel_id=1, source_target_pairs={{0,28},{4,0},{8,4},{12,8},{16,12},{20,16},{24,20},{28,24},{1,29},{... | collective-permute-start | bytes 294920 | tf_op jit(solution)/shard_map/ppermute | solution.py:117
  22.6 3.9 %copy-start.1 = (bf16[1024,512]{1,0:T(8,128)(2,1)S(1)}, bf16[1024,512]{1,0:T(8,128)(2,1)}, u32[]{:S(2)}) copy-start(bf16[1024,512]{1,0:T(8,128)(2,1)} %param.14) | copy-start | bytes 3145732
  24.8 2.8 %copy-start.2 = (bf16[128,1024]{1,0:T(8,128)(2,1)S(1)}, bf16[128,1024]{1,0:T(8,128)(2,1)}, u32[]{:S(2)}) copy-start(bf16[128,1024]{1,0:T(8,128)(2,1)} %param.9) | copy-start | bytes 786436
  27.6 8.7 %collective-permute-start.2 = (bf16[128,1024]{1,0:T(8,128)(2,1)S(1)}, bf16[128,1024]{1,0:T(8,128)(2,1)}, u32[]{:S(2)}, u32[]{:S(2)}) collective-permute-start(bf16[128,1024]{1,0:T(8,128)(2,1)S(1)} %copy-done.2), channel_id=1, source_target_pairs={{0,3},{1,2},{2,1},{3,0},{4,7},{5,6},{6,5},{7,4},{8,11},{9,10},{10,... | collective-permute-start | bytes 786440 | tf_op jit(solution)/shard_map/ppermute | solution.py:96
  27.6 15.7 %collective-permute-start.1 = (bf16[128,1024]{1,0:T(8,128)(2,1)S(1)}, bf16[128,1024]{1,0:T(8,128)(2,1)}, u32[]{:S(2)}, u32[]{:S(2)}) collective-permute-start(bf16[128,1024]{1,0:T(8,128)(2,1)S(1)} %copy-done.2), channel_id=1, source_target_pairs={{0,2},{1,3},{2,0},{3,1},{4,6},{5,7},{6,4},{7,5},{8,10},{9,11},{10,... | collective-permute-start | bytes 786440 | tf_op jit(solution)/shard_map/ppermute | solution.py:96
  28.2 17.3 %collective-permute-start = (bf16[128,1024]{1,0:T(8,128)(2,1)S(1)}, bf16[128,1024]{1,0:T(8,128)(2,1)S(1)}, u32[]{:S(2)}, u32[]{:S(2)}) collective-permute-start(bf16[128,1024]{1,0:T(8,128)(2,1)S(1)} %copy-done.2), channel_id=1, source_target_pairs={{0,1},{1,0},{2,3},{3,2},{4,5},{5,4},{6,7},{7,6},{8,9},{9,8},{10,11... | collective-permute-start | bytes 786440 | tf_op jit(solution)/shard_map/ppermute | solution.py:96
  30.1 18.8 %collective-permute-start.18 = (bf16[128,1024]{1,0:T(8,128)(2,1)}, bf16[128,1024]{1,0:T(8,128)(2,1)}, u32[]{:S(2)}, u32[]{:S(2)}) collective-permute-start(bf16[128,1024]{1,0:T(8,128)(2,1)} %param.10), channel_id=1, source_target_pairs={{0,0},{1,8},{2,16},{3,24},{4,4},{5,12},{6,20},{7,28},{8,1},{9,9},{... | collective-permute-start | bytes 786440 | tf_op jit(solution)/shard_map/ppermute | solution.py:108
  36.3 14.8 %collective-permute-start.7 = (bf16[512,192]{0,1:T(8,128)(2,1)S(1)}, bf16[512,192]{0,1:T(8,128)(2,1)S(1)}, u32[]{:S(2)}, u32[]{:S(2)}) collective-permute-start(bf16[512,192]{0,1:T(8,128)(2,1)S(1)} %bitcast.108), channel_id=1, source_target_pairs={{0,1},{1,0},{2,3},{3,2},{4,5},{5,4},{6,7},{7,6},{8,9},{9,8},{10,11... | collective-permute-start | bytes 589832 | tf_op jit(solution)/shard_map/ppermute | solution.py:96
  43.4 8.2 %collective-permute-start.8 = (bf16[512,192]{0,1:T(8,128)(2,1)S(1)}, bf16[512,192]{0,1:T(8,128)(2,1)S(1)}, u32[]{:S(2)}, u32[]{:S(2)}) collective-permute-start(bf16[512,192]{0,1:T(8,128)(2,1)S(1)} %bitcast.109), channel_id=1, source_target_pairs={{0,2},{1,3},{2,0},{3,1},{4,6},{5,7},{6,4},{7,5},{8,10},{9,11},{10,... | collective-permute-start | bytes 589832 | tf_op jit(solution)/shard_map/ppermute | solution.py:96
  45.5 10.8 %collective-permute-start.9 = (bf16[512,192]{0,1:T(8,128)(2,1)S(1)}, bf16[512,192]{0,1:T(8,128)(2,1)S(1)}, u32[]{:S(2)}, u32[]{:S(2)}) collective-permute-start(bf16[512,192]{0,1:T(8,128)(2,1)S(1)} %bitcast.110), channel_id=1, source_target_pairs={{0,3},{1,2},{2,1},{3,0},{4,7},{5,6},{6,5},{7,4},{8,11},{9,10},{10,... | collective-permute-start | bytes 589832 | tf_op jit(solution)/shard_map/ppermute | solution.py:96
  48.9 20.1 %collective-permute-start.21 = (bf16[128,1024]{1,0:T(8,128)(2,1)}, bf16[128,1024]{1,0:T(8,128)(2,1)S(1)}, u32[]{:S(2)}, u32[]{:S(2)}) collective-permute-start(bf16[128,1024]{1,0:T(8,128)(2,1)} %collective-permute-done.18), channel_id=1, source_target_pairs={{0,3},{1,2},{2,1},{3,0},{4,7},{5,6},{6,5},{7,4},{8,11},{9,10},{10,... | collective-permute-start | bytes 786440 | tf_op jit(solution)/shard_map/ppermute | solution.py:96
  51.1 21.6 %collective-permute-start.20 = (bf16[128,1024]{1,0:T(8,128)(2,1)}, bf16[128,1024]{1,0:T(8,128)(2,1)S(1)}, u32[]{:S(2)}, u32[]{:S(2)}) collective-permute-start(bf16[128,1024]{1,0:T(8,128)(2,1)} %collective-permute-done.18), channel_id=1, source_target_pairs={{0,2},{1,3},{2,0},{3,1},{4,6},{5,7},{6,4},{7,5},{8,10},{9,11},{10,... | collective-permute-start | bytes 786440 | tf_op jit(solution)/shard_map/ppermute | solution.py:96
  51.6 21.1 %collective-permute-start.19 = (bf16[128,1024]{1,0:T(8,128)(2,1)}, bf16[128,1024]{1,0:T(8,128)(2,1)S(1)}, u32[]{:S(2)}, u32[]{:S(2)}) collective-permute-start(bf16[128,1024]{1,0:T(8,128)(2,1)} %collective-permute-done.18), channel_id=1, source_target_pairs={{0,1},{1,0},{2,3},{3,2},{4,5},{5,4},{6,7},{7,6},{8,9},{9,8},{10,11... | collective-permute-start | bytes 786440 | tf_op jit(solution)/shard_map/ppermute | solution.py:96
  56.5 1.4 copy-start.3
  65.8 11.4 %collective-permute-start.12 = (bf16[128,1024]{1,0:T(8,128)(2,1)S(1)}, bf16[128,1024]{1,0:T(8,128)(2,1)S(1)}, u32[]{:S(2)}, u32[]{:S(2)}) collective-permute-start(bf16[128,1024]{1,0:T(8,128)(2,1)S(1)} %shard_map.112), channel_id=1, source_target_pairs={{0,24},{4,28},{8,16},{12,20},{16,8},{20,12},{24,0},{28,4},{1,25},{... | collective-permute-start | bytes 786440 | tf_op jit(solution)/shard_map/ppermute | solution.py:99
  65.9 36.0 %collective-permute-start.11 = (bf16[128,1024]{1,0:T(8,128)(2,1)S(1)}, bf16[128,1024]{1,0:T(8,128)(2,1)S(1)}, u32[]{:S(2)}, u32[]{:S(2)}) collective-permute-start(bf16[128,1024]{1,0:T(8,128)(2,1)S(1)} %shard_map.112), channel_id=1, source_target_pairs={{0,16},{4,20},{8,24},{12,28},{16,0},{20,4},{24,8},{28,12},{1,17},{... | collective-permute-start | bytes 786440 | tf_op jit(solution)/shard_map/ppermute | solution.py:99
  69.0 32.9 %collective-permute-start.10 = (bf16[128,1024]{1,0:T(8,128)(2,1)S(1)}, bf16[128,1024]{1,0:T(8,128)(2,1)S(1)}, u32[]{:S(2)}, u32[]{:S(2)}) collective-permute-start(bf16[128,1024]{1,0:T(8,128)(2,1)S(1)} %shard_map.112), channel_id=1, source_target_pairs={{0,8},{4,12},{8,0},{12,4},{16,24},{20,28},{24,16},{28,20},{1,9},{5... | collective-permute-start | bytes 786440 | tf_op jit(solution)/shard_map/ppermute | solution.py:99
  75.7 30.3 %collective-permute-start.24 = (bf16[128,1024]{1,0:T(8,128)(2,1)S(1)}, bf16[128,1024]{1,0:T(8,128)(2,1)S(1)}, u32[]{:S(2)}, u32[]{:S(2)}) collective-permute-start(bf16[128,1024]{1,0:T(8,128)(2,1)S(1)} %get-tuple-element.13), channel_id=1, source_target_pairs={{0,24},{4,28},{8,16},{12,20},{16,8},{20,12},{24,0},{28,4},{1,25},{... | collective-permute-start | bytes 786440 | tf_op jit(solution)/shard_map/ppermute | solution.py:99
  75.9 36.2 %collective-permute-start.23 = (bf16[128,1024]{1,0:T(8,128)(2,1)S(1)}, bf16[128,1024]{1,0:T(8,128)(2,1)S(1)}, u32[]{:S(2)}, u32[]{:S(2)}) collective-permute-start(bf16[128,1024]{1,0:T(8,128)(2,1)S(1)} %get-tuple-element.14), channel_id=1, source_target_pairs={{0,16},{4,20},{8,24},{12,28},{16,0},{20,4},{24,8},{28,12},{1,17},{... | collective-permute-start | bytes 786440 | tf_op jit(solution)/shard_map/ppermute | solution.py:99
  77.3 45.0 %slice-start = ((s8[8388608]{0:T(1024)(128)(4,1)}), s8[4194304]{0:T(1024)(128)(4,1)S(1)}, s32[]{:S(2)}) async-start(s8[8388608]{0:T(1024)(128)(4,1)} %bitcast.98), calls=%async_computation | async-start | bytes 8388608
  77.3 45.0 %slice-start.1 = ((s8[8388608]{0:T(1024)(128)(4,1)}), s8[4194304]{0:T(1024)(128)(4,1)S(1)}, s32[]{:S(2)}) async-start(s8[8388608]{0:T(1024)(128)(4,1)} %bitcast.98), calls=%async_computation.1 | async-start | bytes 8388608
  77.3 34.8 %collective-permute-start.22 = (bf16[128,1024]{1,0:T(8,128)(2,1)S(1)}, bf16[128,1024]{1,0:T(8,128)(2,1)S(1)}, u32[]{:S(2)}, u32[]{:S(2)}) collective-permute-start(bf16[128,1024]{1,0:T(8,128)(2,1)S(1)} %get-tuple-element.12), channel_id=1, source_target_pairs={{0,8},{4,12},{8,0},{12,4},{16,24},{20,28},{24,16},{28,20},{1,9},{5... | collective-permute-start | bytes 786440 | tf_op jit(solution)/shard_map/ppermute | solution.py:99
  104.8 21.3 %collective-permute-start.16 = (bf16[128,1024]{1,0:T(8,128)(2,1)S(1)}, bf16[128,1024]{1,0:T(8,128)(2,1)S(1)}, u32[]{:S(2)}, u32[]{:S(2)}) collective-permute-start(bf16[128,1024]{1,0:T(8,128)(2,1)S(1)} %get-tuple-element.16), channel_id=1, source_target_pairs={{0,3},{1,2},{2,1},{3,0},{4,7},{5,6},{6,5},{7,4},{8,11},{9,10},{10,... | collective-permute-start | bytes 786440 | tf_op jit(solution)/shard_map/ppermute | solution.py:96
  106.1 20.1 %collective-permute-start.15 = (bf16[128,1024]{1,0:T(8,128)(2,1)S(1)}, bf16[128,1024]{1,0:T(8,128)(2,1)S(1)}, u32[]{:S(2)}, u32[]{:S(2)}) collective-permute-start(bf16[128,1024]{1,0:T(8,128)(2,1)S(1)} %get-tuple-element.17), channel_id=1, source_target_pairs={{0,2},{1,3},{2,0},{3,1},{4,6},{5,7},{6,4},{7,5},{8,10},{9,11},{10,... | collective-permute-start | bytes 786440 | tf_op jit(solution)/shard_map/ppermute | solution.py:96
  106.1 20.1 %collective-permute-start.14 = (bf16[128,1024]{1,0:T(8,128)(2,1)S(1)}, bf16[128,1024]{1,0:T(8,128)(2,1)S(1)}, u32[]{:S(2)}, u32[]{:S(2)}) collective-permute-start(bf16[128,1024]{1,0:T(8,128)(2,1)S(1)} %get-tuple-element.15), channel_id=1, source_target_pairs={{0,1},{1,0},{2,3},{3,2},{4,5},{5,4},{6,7},{7,6},{8,9},{9,8},{10,11... | collective-permute-start | bytes 786440 | tf_op jit(solution)/shard_map/ppermute | solution.py:96
  126.4 36.7 %collective-permute-start.17 = (bf16[128,1024]{1,0:T(8,128)(2,1)S(1)}, bf16[128,1024]{1,0:T(8,128)(2,1)S(1)}, u32[]{:S(2)}, u32[]{:S(2)}) collective-permute-start(bf16[128,1024]{1,0:T(8,128)(2,1)S(1)} %fusion.68), channel_id=1, source_target_pairs={{0,0},{1,8},{2,16},{3,24},{4,4},{5,12},{6,20},{7,28},{8,1},{9,9},{... | collective-permute-start | bytes 786440 | tf_op jit(solution)/shard_map/ppermute | solution.py:108
  128.5 27.8 %collective-permute-start.27 = (bf16[128,1024]{1,0:T(8,128)(2,1)}, bf16[128,1024]{1,0:T(8,128)(2,1)S(1)}, u32[]{:S(2)}, u32[]{:S(2)}) collective-permute-start(bf16[128,1024]{1,0:T(8,128)(2,1)} %fusion.40), channel_id=1, source_target_pairs={{0,3},{1,2},{2,1},{3,0},{4,7},{5,6},{6,5},{7,4},{8,11},{9,10},{10,... | collective-permute-start | bytes 786440 | tf_op jit(solution)/shard_map/ppermute | solution.py:96
  132.1 14.3 %collective-permute-start.30 = (bf16[512,192]{1,0:T(8,128)(2,1)S(1)}, bf16[512,192]{1,0:T(8,128)(2,1)S(1)}, u32[]{:S(2)}, u32[]{:S(2)}) collective-permute-start(bf16[512,192]{1,0:T(8,128)(2,1)S(1)} %get-tuple-element.10), channel_id=1, source_target_pairs={{0,3},{1,2},{2,1},{3,0},{4,7},{5,6},{6,5},{7,4},{8,11},{9,10},{10,... | collective-permute-start | bytes 589832 | tf_op jit(solution)/shard_map/ppermute | solution.py:96
  133.0 21.9 %collective-permute-start.29 = (bf16[512,192]{1,0:T(8,128)(2,1)S(1)}, bf16[512,192]{1,0:T(8,128)(2,1)S(1)}, u32[]{:S(2)}, u32[]{:S(2)}) collective-permute-start(bf16[512,192]{1,0:T(8,128)(2,1)S(1)} %get-tuple-element.11), channel_id=1, source_target_pairs={{0,2},{1,3},{2,0},{3,1},{4,6},{5,7},{6,4},{7,5},{8,10},{9,11},{10,... | collective-permute-start | bytes 589832 | tf_op jit(solution)/shard_map/ppermute | solution.py:96
  135.8 19.1 %collective-permute-start.28 = (bf16[512,192]{1,0:T(8,128)(2,1)S(1)}, bf16[512,192]{1,0:T(8,128)(2,1)S(1)}, u32[]{:S(2)}, u32[]{:S(2)}) collective-permute-start(bf16[512,192]{1,0:T(8,128)(2,1)S(1)} %get-tuple-element.9), channel_id=1, source_target_pairs={{0,1},{1,0},{2,3},{3,2},{4,5},{5,4},{6,7},{7,6},{8,9},{9,8},{10,11... | collective-permute-start | bytes 589832 | tf_op jit(solution)/shard_map/ppermute | solution.py:96
  146.4 13.6 %collective-permute-start.26 = (bf16[128,1024]{1,0:T(8,128)(2,1)}, bf16[128,1024]{1,0:T(8,128)(2,1)}, u32[]{:S(2)}, u32[]{:S(2)}) collective-permute-start(bf16[128,1024]{1,0:T(8,128)(2,1)} %fusion.37), channel_id=1, source_target_pairs={{0,2},{1,3},{2,0},{3,1},{4,6},{5,7},{6,4},{7,5},{8,10},{9,11},{10,... | collective-permute-start | bytes 786440 | tf_op jit(solution)/shard_map/ppermute | solution.py:96
  154.9 5.2 %collective-permute-start.25 = (bf16[128,1024]{1,0:T(8,128)(2,1)}, bf16[128,1024]{1,0:T(8,128)(2,1)}, u32[]{:S(2)}, u32[]{:S(2)}) collective-permute-start(bf16[128,1024]{1,0:T(8,128)(2,1)} %fusion.34), channel_id=1, source_target_pairs={{0,1},{1,0},{2,3},{3,2},{4,5},{5,4},{6,7},{7,6},{8,9},{9,8},{10,11... | collective-permute-start | bytes 786440 | tf_op jit(solution)/shard_map/ppermute | solution.py:96
  155.2 12.5 %collective-permute-start.31 = (bf16[2,128,192]{1,2,0:T(8,128)(2,1)S(1)}, bf16[2,128,192]{1,2,0:T(8,128)(2,1)S(1)}, u32[]{:S(2)}, u32[]{:S(2)}) collective-permute-start(bf16[2,128,192]{1,2,0:T(8,128)(2,1)S(1)} %copy.26), channel_id=1, source_target_pairs={{0,16},{4,20},{8,24},{12,28},{16,0},{20,4},{24,8},{28,12},{1,17},{... | collective-permute-start | bytes 294920 | tf_op jit(solution)/shard_map/ppermute | solution.py:206
  156.3 15.0 %collective-permute-start.32 = (bf16[2,128,192]{1,2,0:T(8,128)(2,1)}, bf16[2,128,192]{1,2,0:T(8,128)(2,1)S(1)}, u32[]{:S(2)}, u32[]{:S(2)}) collective-permute-start(bf16[2,128,192]{1,2,0:T(8,128)(2,1)} %copy.27), channel_id=1, source_target_pairs={{0,12},{4,16},{8,20},{12,24},{16,28},{20,0},{24,4},{28,8},{1,13},{... | collective-permute-start | bytes 294920 | tf_op jit(solution)/shard_map/ppermute | solution.py:206
  160.0 11.3 %collective-permute-start.33 = (bf16[2,128,192]{1,2,0:T(8,128)(2,1)S(1)}, bf16[2,128,192]{1,2,0:T(8,128)(2,1)S(1)}, u32[]{:S(2)}, u32[]{:S(2)}) collective-permute-start(bf16[2,128,192]{1,2,0:T(8,128)(2,1)S(1)} %copy.28), channel_id=1, source_target_pairs={{0,8},{4,12},{8,16},{12,20},{16,24},{20,28},{24,0},{28,4},{1,9},{5... | collective-permute-start | bytes 294920 | tf_op jit(solution)/shard_map/ppermute | solution.py:206
  160.1 11.2 %collective-permute-start.34 = (bf16[2,128,192]{1,2,0:T(8,128)(2,1)S(1)}, bf16[2,128,192]{1,2,0:T(8,128)(2,1)S(1)}, u32[]{:S(2)}, u32[]{:S(2)}) collective-permute-start(bf16[2,128,192]{1,2,0:T(8,128)(2,1)S(1)} %copy.29), channel_id=1, source_target_pairs={{0,4},{4,8},{8,12},{12,16},{16,20},{20,24},{24,28},{28,0},{1,5},{5... | collective-permute-start | bytes 294920 | tf_op jit(solution)/shard_map/ppermute | solution.py:206

commit v2 on v0

v2 whole, which is shorter than its diff:
```python
import functools
import math

import jax
import jax.numpy as jnp
from jax import lax
from jax.experimental import pallas as pl
from jax.experimental.pallas import tpu as pltpu
from jax.sharding import PartitionSpec as P

HEADS = 32
SPAN = 64
K_NB = 2
CAP = 2
WINDOW = 4
BF = jnp.bfloat16
F32 = jnp.float32


def dot_nt(left, right):
    return lax.dot_general(left, right, (((1,), (1,)), ((), ())), preferred_element_type=F32)


def dot_tn(left, right):
    return lax.dot_general(left, right, (((0,), (0,)), ((), ())), preferred_element_type=F32)


def dot(left, right):
    return jnp.dot(left, right, preferred_element_type=F32)


MESH = pl.DeviceIdType.MESH


def kernel(
    dp_count,
    tp,
    owner_ref,
    target_ref,
    hidden_ref,
    grad_ref,
    states_ref,
    wq_hbm,
    kw_hbm,
    vw_hbm,
    ow_hbm,
    cross_ref,
    gh_ref,
    gst_ref,
    wq,
    kw,
    vw,
    w,
    hid,
    turned,
    ga_send,
    ga_recv,
    out_blocks,
    arrived,
    nb,
    q_s,
    k_s,
    v_s,
    att,
    probs_s,
    ga_s,
    gq_s,
    gk_s,
    gv_s,
    st_send,
    st_recv,
    rows_s,
    ret_send,
    ret_recv,
    hp_send,
    hp_recv,
    cp_send,
    cp_recv,
    co_mine,
    co_last,
    send_sem,
    recv_sem,
    local_sem,
):
    g = dp_count // tp
    d, t = lax.axis_index("dp"), lax.axis_index("tensor")
    zz, gx = d // g, d % g
    tokens, width = hidden_ref.shape
    block_count, block_len, width_part = states_ref.shape
    rows_all = block_count * block_len
    pair_rows = CAP * block_len
    pairs = block_count // CAP
    cols = w.shape[2]
    local = q_s.shape[1]
    head_size = local * tp // HEADS
    scale = 1.0 / math.sqrt(head_size)
    spans = tokens // SPAN
    keys = K_NB * block_len

    def tensor_peer(k):
        return (d, (t + k) % tp)

    def zz_peer(j):
        return ((zz + j) % tp * g + gx, t)

    def group_peer(k):
        return (zz * g + (gx + k) % g, t)

    def dp_peer(o):
        return ((d + o + dp_count) % dp_count, t)

    turn_peer = (t * g + gx, zz)
    on_diagonal = t == zz

    local_copies = []

    def load(src, dst):
        copy = pltpu.make_async_copy(src, dst, local_sem.at[len(local_copies)])
        copy.start()
        local_copies.append(copy)
        return copy

    load_w = load(ow_hbm, w.at[gx])
    load_q, load_k, load_v = [], [], []
    for k in range(tp):
        load_q.append(load(wq_hbm.at[pl.ds((t + tp - k) % tp * width, width), :], wq.at[k]))
    for k in range(tp):
        rows = pl.ds((t + tp - k) % tp * width_part, width_part)
        load_k.append(load(kw_hbm.at[rows, :], kw.at[k]))
        load_v.append(load(vw_hbm.at[rows, :], vw.at[k]))

    barrier = pltpu.get_barrier_semaphore()
    peers = [tensor_peer(k) for k in range(1, tp)] + [zz_peer(j) for j in range(1, tp)]
    peers += [group_peer(k) for k in range(1, g)]
    peers += [dp_peer(o) for o in range(1, WINDOW + 1)]
    peers += [dp_peer(-o) for o in range(1, WINDOW + 1)]
    peers.append(turn_peer)
    for peer in peers:
        pl.semaphore_signal(barrier, inc=1, device_id=peer, device_id_type=MESH)
    pl.semaphore_wait(barrier, len(peers))

    sent = []
    used = [0]

    def remote(src, dst, peer):
        i = used[0]
        used[0] += 1
        return pltpu.make_async_remote_copy(
            src_ref=src,
            dst_ref=dst,
            send_sem=send_sem.at[i],
            recv_sem=recv_sem.at[i],
            device_id=peer,
            device_id_type=MESH,
        )

    def send(src, dst, peer):
        copy = remote(src, dst, peer)
        copy.start()
        sent.append(copy)
        return copy

    def is_gap(gap, o):
        return jnp.where(gap == o, 1.0, 0.0).astype(F32)

    owner_gap = [(owner_ref[0, k * CAP] - d + dp_count) % dp_count for k in range(pairs)]
    target_gap = [(d - target_ref[0, k * CAP] + dp_count) % dp_count for k in range(pairs)]

    for o in range(1, WINDOW + 1):
        block = sum(
            is_gap(target_gap[k], o)
            * states_ref[pl.ds(k * CAP, CAP)].astype(F32).reshape(pair_rows, width_part)
            for k in range(pairs)
        )
        out_blocks[o - 1] = block.astype(BF)
    blocks_in = [
        send(out_blocks.at[o - 1], arrived.at[o - 1], dp_peer(-o)) for o in range(1, WINDOW + 1)
    ]
    turn_in = remote(grad_ref, turned.at[0], turn_peer)

    @pl.when(jnp.logical_not(on_diagonal))
    def _():
        turn_in.start()

    @pl.when(on_diagonal)
    def _():
        turned[0] = grad_ref[...]

    hidden_in = [None] + [send(hidden_ref, hid.at[k], tensor_peer(k)) for k in range(1, tp)]
    weight_in = [send(ow_hbm, w.at[gx], group_peer(k)) for k in range(1, g)]

    for copy in blocks_in:
        copy.wait_recv()
    for k in range(pairs):
        block = sum(
            is_gap(owner_gap[k], o) * arrived[o - 1].astype(F32) for o in range(1, WINDOW + 1)
        )
        nb[0, pl.ds(k * pair_rows, pair_rows), :] = block.astype(BF)
    nb_in = [None] + [send(nb.at[0], nb.at[k], tensor_peer(k)) for k in range(1, tp)]

    @pl.when(jnp.logical_not(on_diagonal))
    def _():
        turn_in.wait()

    turned_in = [send(turned.at[0], turned.at[k], tensor_peer(k)) for k in range(1, tp)]

    hid[0] = hidden_ref[...]
    for k in range(1, tp):
        hidden_in[k].wait_recv()
    for copy in load_q:
        copy.wait()
    tile = min(256, local)
    for c in range(0, local, tile):
        at = pl.ds(c, tile)
        q_s[:, at] = sum(dot(hid[k], wq[k, :, at]) for k in range(tp)).astype(BF)

    load_w.wait()
    for copy in weight_in + turned_in:
        copy.wait_recv()

    def ga_partial(j):
        block = turned[(t - zz - j + 2 * tp) % tp]
        return sum(
            dot_nt(block[:, m * cols : (m + 1) * cols], w[m]) for m in range(g)
        )

    ga_in = []
    for j in range(1, tp):
        ga_send[j] = ga_partial(j).astype(BF)
        ga_in.append(send(ga_send.at[j], ga_recv.at[j], zz_peer(j)))
    ga_send[0] = ga_partial(0).astype(BF)

    for k in range(1, tp):
        nb_in[k].wait_recv()
    for copy in load_k + load_v:
        copy.wait()
    for c in range(0, local, tile):
        at = pl.ds(c, tile)
        k_s[:, at] = sum(dot(nb[k], kw[k, :, at]) for k in range(tp)).astype(BF)
        v_s[:, at] = sum(dot(nb[k], vw[k, :, at]) for k in range(tp)).astype(BF)

    heads = local // head_size

    def forward(h, carry):
        at = pl.ds(pl.multiple_of(h * head_size, head_size), head_size)
        for c in range(spans):
            mine, theirs = pl.ds(c * SPAN, SPAN), pl.ds(c * keys, keys)
            scores = dot_nt(q_s[mine, at], k_s[theirs, at]) * scale
            expanded = jnp.exp(scores - jnp.max(scores, axis=-1, keepdims=True))
            probs = expanded / jnp.sum(expanded, axis=-1, keepdims=True)
            probs_s[h, mine, :] = probs
            att[0, mine, at] = dot(probs.astype(BF), v_s[theirs, at]).astype(BF)
        return carry

    lax.fori_loop(0, heads, forward, 0)
    att_in = [send(att.at[0], att.at[j], zz_peer(j)) for j in range(1, tp)]

    for copy in ga_in:
        copy.wait_recv()
    total = ga_send[0].astype(F32)
    for j in range(1, tp):
        total += ga_recv[j].astype(F32)
    ga_s[...] = total.astype(BF)

    def backward(h, carry):
        at = pl.ds(pl.multiple_of(h * head_size, head_size), head_size)
        for c in range(spans):
            mine, theirs = pl.ds(c * SPAN, SPAN), pl.ds(c * keys, keys)
            probs, ga = probs_s[h, mine, :], ga_s[mine, at]
            gp = dot_nt(ga, v_s[theirs, at])
            gs = (probs * (gp - jnp.sum(probs * gp, axis=-1, keepdims=True)) * scale).astype(BF)
            gq_s[mine, at] = dot(gs, k_s[theirs, at]).astype(BF)
            gk_s[theirs, at] = dot_tn(gs, q_s[mine, at]).astype(BF)
            gv_s[theirs, at] = dot_tn(probs.astype(BF), ga).astype(BF)
        return carry

    lax.fori_loop(0, heads, backward, 0)

    def states_partial(k):
        slot = (tp - k) % tp
        return dot_nt(gk_s[...], kw[slot]) + dot_nt(gv_s[...], vw[slot])

    st_in = []
    for k in range(1, tp):
        st_send[k] = states_partial(k).astype(BF)
        st_in.append(send(st_send.at[k], st_recv.at[k], tensor_peer(k)))
    st_send[0] = states_partial(0).astype(BF)

    for copy in att_in:
        copy.wait_recv()

    def cross_partial(k):
        block = att[(zz - t - k + 2 * tp) % tp]
        for m in range(g):
            cp_send[k, :, m * cols : (m + 1) * cols] = dot(block, w[m]).astype(BF)

    cp_in = []
    for k in range(1, tp):
        cross_partial(k)
        cp_in.append(send(cp_send.at[k], cp_recv.at[k], tensor_peer(k)))
    cross_partial(0)

    def hidden_partial(k):
        return dot_nt(gq_s[...], wq[(tp - k) % tp])

    hp_in = []
    for k in range(1, tp):
        hp_send[k] = hidden_partial(k).astype(BF)
        hp_in.append(send(hp_send.at[k], hp_recv.at[k], tensor_peer(k)))

    for copy in st_in:
        copy.wait_recv()
    total = st_send[0].astype(F32)
    for k in range(1, tp):
        total += st_recv[k].astype(F32)
    rows_s[...] = total.astype(BF)
    for o in range(1, WINDOW + 1):
        block = sum(
            is_gap(owner_gap[k], o) * rows_s[pl.ds(k * pair_rows, pair_rows), :].astype(F32)
            for k in range(pairs)
        )
        ret_send[o - 1] = block.astype(BF)
    ret_in = [
        send(ret_send.at[o - 1], ret_recv.at[o - 1], dp_peer(o)) for o in range(1, WINDOW + 1)
    ]

    for copy in cp_in:
        copy.wait_recv()
    total = cp_send[0].astype(F32)
    for k in range(1, tp):
        total += cp_recv[k].astype(F32)
    co_mine[...] = total.astype(BF)
    cross_in = remote(co_mine, co_last, turn_peer)

    @pl.when(jnp.logical_not(on_diagonal))
    def _():
        cross_in.start()

    @pl.when(on_diagonal)
    def _():
        co_last[...] = co_mine[...]

    total = hidden_partial(0).astype(BF).astype(F32)
    for copy in hp_in:
        copy.wait_recv()
    for k in range(1, tp):
        total += hp_recv[k].astype(F32)
    gh_ref[...] = total.astype(BF)

    for copy in ret_in:
        copy.wait_recv()
    for k in range(pairs):
        block = sum(
            is_gap(target_gap[k], o) * ret_recv[o - 1].astype(F32) for o in range(1, WINDOW + 1)
        )
        gst_ref[pl.ds(k * CAP, CAP)] = block.astype(BF).reshape(CAP, block_len, width_part)

    @pl.when(jnp.logical_not(on_diagonal))
    def _():
        cross_in.wait()

    cross_ref[...] = co_last[...]
    for copy in sent:
        copy.wait_send()


def shards(
    hidden,
    grad_out,
    query_weight,
    key_weight,
    value_weight,
    out_weight,
    neighbour_states,
    block_owner,
    slot_target,
):
    dp_count, tp = lax.axis_size("dp"), lax.axis_size("tensor")
    g = dp_count // tp
    tokens, width = hidden.shape
    local = query_weight.shape[1]
    block_count, block_len, width_part = neighbour_states.shape
    rows = block_count * block_len
    pair_rows = CAP * block_len
    heads = HEADS // tp
    copies = 2 * WINDOW + 8 * (tp - 1) + (g - 1) + 2

    def vmem(*shape, kind=BF):
        return pltpu.VMEM(shape, kind)

    in_vmem = pl.BlockSpec(memory_space=pltpu.VMEM)
    in_smem = pl.BlockSpec(memory_space=pltpu.SMEM)
    anywhere = pl.BlockSpec(memory_space=pl.ANY)
    multiply_adds = tokens * tp * width * local * 4 + rows * local * tp * width_part * 4
    return pl.pallas_call(
        functools.partial(kernel, dp_count, tp),
        in_specs=[in_smem] * 2 + [in_vmem] * 3 + [anywhere] * 4,
        out_specs=[in_vmem] * 3,
        out_shape=[
            jax.ShapeDtypeStruct(hidden.shape, BF),
            jax.ShapeDtypeStruct(hidden.shape, BF),
            jax.ShapeDtypeStruct(neighbour_states.shape, BF),
        ],
        scratch_shapes=[
            vmem(tp, width, local),
            vmem(tp, width_part, local),
            vmem(tp, width_part, local),
            vmem(g, *out_weight.shape),
            vmem(tp, tokens, width),
            vmem(tp, tokens, width),
            vmem(tp, tokens, local),
            vmem(tp, tokens, local),
            vmem(WINDOW, pair_rows, width_part),
            vmem(WINDOW, pair_rows, width_part),
            vmem(tp, rows, width_part),
            vmem(tokens, local),
            vmem(rows, local),
            vmem(rows, local),
            vmem(tp, tokens, local),
            vmem(heads, tokens, K_NB * block_len, kind=F32),
            vmem(tokens, local),
            vmem(tokens, local),
            vmem(rows, local),
            vmem(rows, local),
            vmem(tp, rows, width_part),
            vmem(tp, rows, width_part),
            vmem(rows, width_part),
            vmem(WINDOW, pair_rows, width_part),
            vmem(WINDOW, pair_rows, width_part),
            vmem(tp, tokens, width),
            vmem(tp, tokens, width),
            vmem(tp, tokens, width),
            vmem(tp, tokens, width),
            vmem(tokens, width),
            vmem(tokens, width),
            pltpu.SemaphoreType.DMA((copies,)),
            pltpu.SemaphoreType.DMA((copies,)),
            pltpu.SemaphoreType.DMA((3 * tp + 1,)),
        ],
        cost_estimate=pl.CostEstimate(
            flops=2 * multiply_adds, bytes_accessed=16 * 2**20, transcendentals=0
        ),
        compiler_params=pltpu.CompilerParams(
            collective_id=0, has_side_effects=True, vmem_limit_bytes=52 * 2**20
        ),
    )(
        block_owner,
        slot_target,
        hidden,
        grad_out,
        neighbour_states,
        query_weight,
        key_weight,
        value_weight,
        out_weight,
    )


def solution(mesh):
    placed = (
        P("dp", "tensor"),
        P("dp", "tensor"),
        P(None, "tensor"),
        P(None, "tensor"),
        P(None, "tensor"),
        P("tensor", "dp"),
        P("dp", None, "tensor"),
        P("dp", None),
        P("dp", None),
    )
    return jax.shard_map(
        shards,
        mesh=mesh,
        in_specs=placed,
        out_specs=(P("dp", "tensor"), P("dp", "tensor"), P("dp", None, "tensor")),
        check_vma=False,
    )
```

time: 291 us -> 134 us (0.46)
  the two profiles are of different devices: /device:TPU:4 before, /device:TPU:13 now
where the time goes in v2:
time: 134 us
  Pallas kernels  127 us (95%)
  local copies, waits for them, and re-layouts  6.49 us (5%)
    pallas_call x1, Pallas kernels, shards(): pl.pallas_call(functools.partial(kernel, dp_count, tp), in_specs=[in_smem...  127 us
    unnamed x11, local copies, waits for them, and re-layouts  5.67 us

profile of v2, /device:TPU:13, one launch (start us, length us, event | category | flops | bytes accessed | tf_op | source)
XLA Modules:
  0.0 134.1 jit_solution(6214857089899169638)
XLA Ops:
  0.6 1.1 copy.12.states_ref
  1.7 0.0 copy-start
  1.7 0.9 copy-done
  2.7 0.0 copy-start.1
  2.7 0.9 copy-done.1
  3.6 0.0 copy-start.2
  3.6 0.7 copy-done.2
  4.3 0.0 copy-start.3
  4.3 0.7 copy-done.3
  4.9 127.0 %shard_map.112 = (bf16[128,1024]{1,0:T(8,128)(2,1)S(1)}, bf16[128,1024]{1,0:T(8,128)(2,1)S(1)}, bf16[4,128,192]{2,1,0:T(8,128)(2,1)S(1)}) custom-call(s32[1,4]{1,0:T(1,128)S(1)} %copy-done.2, s32[1,4]{1,0:T(1,128)S(1)} %copy-done.3, bf16[128,1024]{1,0:T(8,128)(2,1)S(1)} %copy-done, bf16[128,1024]{1,0:T(8,128)(2,1)S(1)} %copy-done.1, ...), custom_call_target="tpu_custom_call" | custom-call | flops 7516192768 | bytes 16777216 | tf_op jit(solution)/shard_map/pallas_call | solution.py:395
  131.9 0.8 copy.13
  132.7 0.7 copy.16
  133.4 0.7 copy.17
Async XLA Ops:
  1.7 1.0 copy-start
  2.7 0.9 copy-start.1
  3.6 0.7 copy-start.2
  4.3 0.7 copy-start.3

commit v3 on v2

v3 whole, which is shorter than its diff:
```python
import functools
import math

import jax
import jax.numpy as jnp
from jax import lax
from jax.experimental import pallas as pl
from jax.experimental.pallas import tpu as pltpu
from jax.sharding import PartitionSpec as P

HEADS = 32
SPAN = 64
K_NB = 2
CAP = 2
WINDOW = 4
BF = jnp.bfloat16
F32 = jnp.float32


def dot_nt(left, right):
    return lax.dot_general(left, right, (((1,), (1,)), ((), ())), preferred_element_type=F32)


def dot_tn(left, right):
    return lax.dot_general(left, right, (((0,), (0,)), ((), ())), preferred_element_type=F32)


def dot(left, right):
    return jnp.dot(left, right, preferred_element_type=F32)


MESH = pl.DeviceIdType.MESH
LANES = 128


def flip(i, k):
    if k % 2:
        i = i + 1 - 2 * (i % 2)
    return (i + 2) % 4 if k >= 2 else i


def packed(block):
    half = block.shape[0] // 2
    rest = jnp.concatenate([block[:half, LANES:], block[half:, LANES:]], axis=1)
    return jnp.concatenate([block[:, :LANES], rest], axis=0)


def kernel(
    dp_count,
    tp,
    owner_hbm,
    target_hbm,
    hidden_hbm,
    grad_hbm,
    states_hbm,
    wq_hbm,
    kw_hbm,
    vw_hbm,
    ow_hbm,
    cross_ref,
    gh_ref,
    gst_ref,
    owner_ref,
    target_ref,
    states_ref,
    wq,
    kw,
    vw,
    w,
    hid,
    turned,
    ga_send,
    ga_recv,
    out_blocks,
    arrived,
    nbp,
    nb,
    q_s,
    k_s,
    v_s,
    att,
    probs_s,
    ga_s,
    gq_s,
    gk_s,
    gv_s,
    st_send,
    st_recv,
    rows_s,
    ret_send,
    ret_recv,
    hp_send,
    hp_recv,
    cp_send,
    cp_recv,
    co_mine,
    co_last,
    send_sem,
    recv_sem,
    local_sem,
):
    g = dp_count // tp
    d, t = lax.axis_index("dp"), lax.axis_index("tensor")
    zz, gx = d // g, d % g
    tokens, width = hidden_hbm.shape
    block_count, block_len, width_part = states_ref.shape
    rows_all = block_count * block_len
    pair_rows = CAP * block_len
    pairs = block_count // CAP
    cols = w.shape[2]
    local = q_s.shape[1]
    head_size = local * tp // HEADS
    scale = 1.0 / math.sqrt(head_size)
    spans = tokens // SPAN
    keys = K_NB * block_len

    def tensor_peer(k):
        return (d, flip(t, k))

    def zz_peer(j):
        return (flip(zz, j) * g + gx, t)

    def group_peer(k):
        return (zz * g + (gx + k) % g, t)

    def dp_peer(o):
        return ((d + o + dp_count) % dp_count, t)

    turn_peer = (t * g + gx, zz)
    on_diagonal = t == zz
    apart = (zz + t) % 2 + 2 * ((zz // 2 + t // 2) % 2)

    local_copies = []

    def load(src, dst):
        copy = pltpu.make_async_copy(src, dst, local_sem.at[len(local_copies)])
        copy.start()
        local_copies.append(copy)
        return copy

    load_small = [
        load(owner_hbm, owner_ref),
        load(target_hbm, target_ref),
        load(states_hbm, states_ref),
    ]
    load_hidden = load(hidden_hbm, hid.at[0])
    load_w = load(ow_hbm, w.at[gx])
    load_q, load_kv = [], []
    for k in range(tp):
        load_q.append(load(wq_hbm.at[pl.ds(flip(t, k) * width, width), :], wq.at[k]))
    rest = width_part - LANES
    for k in range(tp):
        for hbm, here in ((kw_hbm, kw), (vw_hbm, vw)):
            start = flip(t, k) * width_part
            for first, size, to in ((0, LANES, k * LANES), (LANES, rest, tp * LANES + k * rest)):
                load_kv.append(
                    load(hbm.at[pl.ds(start + first, size), :], here.at[pl.ds(to, size), :])
                )

    barrier = pltpu.get_barrier_semaphore()
    peers = [tensor_peer(1), tensor_peer(2), zz_peer(1), zz_peer(2)]
    peers += [group_peer(k) for k in range(1, g)]
    peers += [dp_peer(o) for o in range(1, WINDOW + 1)]
    peers += [dp_peer(-o) for o in range(1, WINDOW + 1)]
    peers.append(turn_peer)
    for peer in peers:
        pl.semaphore_signal(barrier, inc=1, device_id=peer, device_id_type=MESH)
    pl.semaphore_wait(barrier, len(peers))

    sent = []
    used = [0]

    def remote(src, dst, peer):
        i = used[0]
        used[0] += 1
        return pltpu.make_async_remote_copy(
            src_ref=src,
            dst_ref=dst,
            send_sem=send_sem.at[i],
            recv_sem=recv_sem.at[i],
            device_id=peer,
            device_id_type=MESH,
        )

    def send(src, dst, peer):
        copy = remote(src, dst, peer)
        copy.start()
        sent.append(copy)
        return copy

    def gather(src, slots, peer):
        return [send(src, slots.at[1], peer(1)), send(src, slots.at[2], peer(2))]

    def forwarded(slots, peer, copies):
        copies[1].wait_recv()
        return send(slots.at[2], slots.at[3], peer(1))

    def scatter_start(parts, recv, peer):
        return [send(parts.at[3], recv.at[1], peer(1)), send(parts.at[1], recv.at[0], peer(1))]

    def scatter_middle(parts, recv, peer, copies):
        copies[0].wait_recv()
        parts[2] = (parts[2].astype(F32) + recv[1].astype(F32)).astype(BF)
        copies.append(send(parts.at[2], recv.at[2], peer(2)))

    def scatter_end(parts, recv, copies):
        copies[1].wait_recv()
        copies[2].wait_recv()
        return parts[0].astype(F32) + recv[0].astype(F32) + recv[2].astype(F32)

    def is_gap(gap, o):
        return jnp.where(gap == o, 1.0, 0.0).astype(F32)

    for copy in load_small:
        copy.wait()
    owner_gap = [(owner_ref[0, k * CAP] - d + dp_count) % dp_count for k in range(pairs)]
    target_gap = [(d - target_ref[0, k * CAP] + dp_count) % dp_count for k in range(pairs)]

    pair_packs = [
        packed(states_ref[pl.ds(k * CAP, CAP)].astype(F32).reshape(pair_rows, width_part))
        for k in range(pairs)
    ]
    blocks_in = []
    for o in range(1, WINDOW + 1):
        block = sum(is_gap(target_gap[k], o) * pair_packs[k] for k in range(pairs))
        out_blocks[o - 1] = block.astype(BF)
        blocks_in.append(send(out_blocks.at[o - 1], arrived.at[o - 1], dp_peer(-o)))
    turn_in = remote(grad_hbm, turned.at[0], turn_peer)
    turn_local = pltpu.make_async_copy(grad_hbm, turned.at[0], local_sem.at[len(local_copies)])

    @pl.when(jnp.logical_not(on_diagonal))
    def _():
        turn_in.start()

    @pl.when(on_diagonal)
    def _():
        turn_local.start()

    hidden_in = gather(hidden_hbm, hid, tensor_peer)
    weight_in = [send(ow_hbm, w.at[gx], group_peer(k)) for k in range(1, g)]

    @pl.when(jnp.logical_not(on_diagonal))
    def _():
        turn_in.wait()

    @pl.when(on_diagonal)
    def _():
        turn_local.wait()

    turned_in = gather(turned.at[0], turned, tensor_peer)

    for copy in blocks_in:
        copy.wait_recv()
    for k in range(pairs):
        block = sum(
            is_gap(owner_gap[k], o) * arrived[o - 1].astype(F32) for o in range(1, WINDOW + 1)
        ).astype(BF)
        nbp[0, pl.ds(k * pair_rows, pair_rows), :] = block[:pair_rows]
        nbp[0, pl.ds(rows_all + k * block_len, block_len), :] = block[pair_rows:]
    nb_in = gather(nbp.at[0], nbp, tensor_peer)

    hidden_in.append(forwarded(hid, tensor_peer, hidden_in))
    turned_in.append(forwarded(turned, tensor_peer, turned_in))
    load_hidden.wait()
    hidden_in[0].wait_recv()
    hidden_in[2].wait_recv()
    for copy in load_q:
        copy.wait()
    tile = min(256, local)
    for c in range(0, local, tile):
        at = pl.ds(c, tile)
        q_s[:, at] = sum(dot(hid[k], wq[k, :, at]) for k in range(tp)).astype(BF)
    nb_in.append(forwarded(nbp, tensor_peer, nb_in))

    load_w.wait()
    for copy in weight_in:
        copy.wait_recv()
    turned_in[0].wait_recv()
    turned_in[2].wait_recv()

    def ga_partial(j):
        block = turned[flip(apart, j)]
        ga_send[j] = sum(
            dot_nt(block[:, m * cols : (m + 1) * cols], w[m]) for m in range(g)
        ).astype(BF)

    ga_partial(3)
    ga_partial(1)
    ga_in = scatter_start(ga_send, ga_recv, zz_peer)
    ga_partial(2)
    ga_partial(0)

    nb_in[0].wait_recv()
    nb_in[2].wait_recv()
    for k in range(tp):
        nb[:, k * LANES : (k + 1) * LANES] = nbp[k, pl.ds(0, rows_all), :]
    for k in range(0, tp, 2):
        for p in range(pairs):
            rows = pl.ds(rows_all + p * block_len, block_len)
            one, two = nbp[k, rows, :].astype(F32), nbp[k + 1, rows, :].astype(F32)
            lanes = pl.ds(tp * LANES + k * rest, 2 * rest)
            for half in range(2):
                part = slice(half * rest, (half + 1) * rest)
                joined = jnp.concatenate([one[:, part], two[:, part]], axis=1)
                nb[pl.ds((p * CAP + half) * block_len, block_len), lanes] = joined.astype(BF)
    for copy in load_kv:
        copy.wait()
    for c in range(0, local, tile):
        at = pl.ds(c, tile)
        k_s[:, at] = dot(nb[...], kw[:, at]).astype(BF)
        v_s[:, at] = dot(nb[...], vw[:, at]).astype(BF)
    scatter_middle(ga_send, ga_recv, zz_peer, ga_in)

    heads = local // head_size

    def forward(h, carry):
        at = pl.ds(pl.multiple_of(h * head_size, head_size), head_size)
        for c in range(spans):
            mine, theirs = pl.ds(c * SPAN, SPAN), pl.ds(c * keys, keys)
            scores = dot_nt(q_s[mine, at], k_s[theirs, at]) * scale
            expanded = jnp.exp(scores - jnp.max(scores, axis=-1, keepdims=True))
            probs = expanded / jnp.sum(expanded, axis=-1, keepdims=True)
            probs_s[h, mine, :] = probs
            att[0, mine, at] = dot(probs.astype(BF), v_s[theirs, at]).astype(BF)
        return carry

    lax.fori_loop(0, heads, forward, 0, unroll=4)
    att_in = gather(att.at[0], att, zz_peer)

    ga_s[...] = scatter_end(ga_send, ga_recv, ga_in).astype(BF)
    att_in.append(forwarded(att, zz_peer, att_in))

    def backward(h, carry):
        at = pl.ds(pl.multiple_of(h * head_size, head_size), head_size)
        for c in range(spans):
            mine, theirs = pl.ds(c * SPAN, SPAN), pl.ds(c * keys, keys)
            probs, ga = probs_s[h, mine, :], ga_s[mine, at]
            gp = dot_nt(ga, v_s[theirs, at])
            gs = (probs * (gp - jnp.sum(probs * gp, axis=-1, keepdims=True)) * scale).astype(BF)
            gq_s[mine, at] = dot(gs, k_s[theirs, at]).astype(BF)
            gk_s[theirs, at] = dot_tn(gs, q_s[mine, at]).astype(BF)
            gv_s[theirs, at] = dot_tn(probs.astype(BF), ga).astype(BF)
        return carry

    lax.fori_loop(0, heads, backward, 0, unroll=4)

    for k in range(0, tp, 2):
        at = pl.ds(k * LANES, 2 * LANES)
        both = dot_nt(gk_s[...], kw[at, :]) + dot_nt(gv_s[...], vw[at, :])
        for i in range(2):
            st_send[k + i, pl.ds(0, rows_all), :] = both[:, i * LANES : (i + 1) * LANES].astype(BF)
    at = pl.ds(tp * LANES, tp * rest)
    both = dot_nt(gk_s[...], kw[at, :]) + dot_nt(gv_s[...], vw[at, :])
    for k in range(tp):
        part = slice(k * rest, (k + 1) * rest)
        for p in range(pairs):
            top = p * pair_rows
            joined = jnp.concatenate(
                [both[top : top + block_len, part], both[top + block_len : top + pair_rows, part]],
                axis=1,
            )
            st_send[k, pl.ds(rows_all + p * block_len, block_len), :] = joined.astype(BF)
    st_in = scatter_start(st_send, st_recv, tensor_peer)

    def cross_partial(k):
        block = att[flip(apart, k)]
        for m in range(g):
            cp_send[k, :, m * cols : (m + 1) * cols] = dot(block, w[m]).astype(BF)

    att_in[0].wait_recv()
    att_in[2].wait_recv()
    cross_partial(3)
    cross_partial(1)
    cp_in = scatter_start(cp_send, cp_recv, tensor_peer)
    scatter_middle(st_send, st_recv, tensor_peer, st_in)
    cross_partial(2)
    scatter_middle(cp_send, cp_recv, tensor_peer, cp_in)
    cross_partial(0)

    def hidden_partial(k):
        hp_send[k] = dot_nt(gq_s[...], wq[k]).astype(BF)

    hidden_partial(3)
    hidden_partial(1)
    hp_in = scatter_start(hp_send, hp_recv, tensor_peer)

    rows_s[...] = scatter_end(st_send, st_recv, st_in).astype(BF)
    ret_in = []
    for o in range(1, WINDOW + 1):
        for first, size, to in ((0, pair_rows, 0), (rows_all, block_len, pair_rows)):
            block = sum(
                is_gap(owner_gap[k], o) * rows_s[pl.ds(first + k * size, size), :].astype(F32)
                for k in range(pairs)
            )
            ret_send[o - 1, pl.ds(to, size), :] = block.astype(BF)
        ret_in.append(send(ret_send.at[o - 1], ret_recv.at[o - 1], dp_peer(o)))

    co_mine[...] = scatter_end(cp_send, cp_recv, cp_in).astype(BF)
    cross_in = remote(co_mine, co_last, turn_peer)

    @pl.when(jnp.logical_not(on_diagonal))
    def _():
        cross_in.start()

    @pl.when(on_diagonal)
    def _():
        co_last[...] = co_mine[...]

    hidden_partial(2)
    scatter_middle(hp_send, hp_recv, tensor_peer, hp_in)
    hidden_partial(0)
    gh_ref[...] = scatter_end(hp_send, hp_recv, hp_in).astype(BF)

    for copy in ret_in:
        copy.wait_recv()
    for k in range(pairs):
        block = sum(
            is_gap(target_gap[k], o) * ret_recv[o - 1].astype(F32) for o in range(1, WINDOW + 1)
        )
        for i in range(CAP):
            gst_ref[k * CAP + i, :, :LANES] = block[i * block_len : (i + 1) * block_len].astype(BF)
            gst_ref[k * CAP + i, :, LANES:] = block[
                pair_rows:, i * rest : (i + 1) * rest
            ].astype(BF)

    @pl.when(jnp.logical_not(on_diagonal))
    def _():
        cross_in.wait()

    cross_ref[...] = co_last[...]
    for copy in sent:
        copy.wait_send()


def shards(
    hidden,
    grad_out,
    query_weight,
    key_weight,
    value_weight,
    out_weight,
    neighbour_states,
    block_owner,
    slot_target,
):
    dp_count, tp = lax.axis_size("dp"), lax.axis_size("tensor")
    g = dp_count // tp
    tokens, width = hidden.shape
    local = query_weight.shape[1]
    block_count, block_len, width_part = neighbour_states.shape
    rows = block_count * block_len
    pack = rows * width_part // LANES
    heads = HEADS // tp
    copies = 2 * WINDOW + 8 * (tp - 1) + (g - 1) + 2

    def vmem(*shape, kind=BF):
        return pltpu.VMEM(shape, kind)

    in_vmem = pl.BlockSpec(memory_space=pltpu.VMEM)
    anywhere = pl.BlockSpec(memory_space=pl.ANY)
    multiply_adds = tokens * tp * width * local * 4 + rows * local * tp * width_part * 4
    return pl.pallas_call(
        functools.partial(kernel, dp_count, tp),
        in_specs=[anywhere] * 9,
        out_specs=[in_vmem] * 3,
        out_shape=[
            jax.ShapeDtypeStruct(hidden.shape, BF),
            jax.ShapeDtypeStruct(hidden.shape, BF),
            jax.ShapeDtypeStruct(neighbour_states.shape, BF),
        ],
        scratch_shapes=[
            pltpu.SMEM(block_owner.shape, jnp.int32),
            pltpu.SMEM(slot_target.shape, jnp.int32),
            vmem(*neighbour_states.shape),
            vmem(tp, width, local),
            vmem(tp * width_part, local),
            vmem(tp * width_part, local),
            vmem(g, *out_weight.shape),
            vmem(tp, tokens, width),
            vmem(tp, tokens, width),
            vmem(tp, tokens, local),
            vmem(tp, tokens, local),
            vmem(WINDOW, 3 * block_len, LANES),
            vmem(WINDOW, 3 * block_len, LANES),
            vmem(tp, pack, LANES),
            vmem(rows, tp * width_part),
            vmem(tokens, local),
            vmem(rows, local),
            vmem(rows, local),
            vmem(tp, tokens, local),
            vmem(heads, tokens, K_NB * block_len, kind=F32),
            vmem(tokens, local),
            vmem(tokens, local),
            vmem(rows, local),
            vmem(rows, local),
            vmem(tp, pack, LANES),
            vmem(tp, pack, LANES),
            vmem(pack, LANES),
            vmem(WINDOW, 3 * block_len, LANES),
            vmem(WINDOW, 3 * block_len, LANES),
            vmem(tp, tokens, width),
            vmem(tp, tokens, width),
            vmem(tp, tokens, width),
            vmem(tp, tokens, width),
            vmem(tokens, width),
            vmem(tokens, width),
            pltpu.SemaphoreType.DMA((copies,)),
            pltpu.SemaphoreType.DMA((copies,)),
            pltpu.SemaphoreType.DMA((5 * tp + 6,)),
        ],
        cost_estimate=pl.CostEstimate(
            flops=2 * multiply_adds, bytes_accessed=16 * 2**20, transcendentals=0
        ),
        compiler_params=pltpu.CompilerParams(
            collective_id=0, has_side_effects=True, vmem_limit_bytes=52 * 2**20
        ),
    )(
        block_owner,
        slot_target,
        hidden,
        grad_out,
        neighbour_states,
        query_weight,
        key_weight,
        value_weight,
        out_weight,
    )


def solution(mesh):
    placed = (
        P("dp", "tensor"),
        P("dp", "tensor"),
        P(None, "tensor"),
        P(None, "tensor"),
        P(None, "tensor"),
        P("tensor", "dp"),
        P("dp", None, "tensor"),
        P("dp", None),
        P("dp", None),
    )
    return jax.shard_map(
        shards,
        mesh=mesh,
        in_specs=placed,
        out_specs=(P("dp", "tensor"), P("dp", "tensor"), P("dp", None, "tensor")),
        check_vma=False,
    )
```

time: 134 us -> 115 us (0.86)
  the two profiles are of different devices: /device:TPU:13 before, /device:TPU:4 now
where the time goes in v3:
time: 115 us; the launch traced here: 114 us
  Pallas kernels  107 us (93%)
  local copies, waits for them, and re-layouts  6.49 us (6%)
    pallas_call x1, Pallas kernels, shards(): pl.pallas_call(functools.partial(kernel, dp_count, tp), in_specs=[anywher...  107 us
    unnamed x11, local copies, waits for them, and re-layouts  5.67 us

profile of v3, /device:TPU:4, one launch (start us, length us, event | category | flops | bytes accessed | tf_op | source)
XLA Modules:
  0.0 114.4 jit_solution(15091252826438311072)
XLA Ops:
  0.6 1.1 copy.12.states_hbm
  1.7 0.0 copy-start
  1.7 0.9 copy-done
  2.7 0.0 copy-start.1
  2.7 0.9 copy-done.1
  3.6 0.0 copy-start.2
  3.6 0.7 copy-done.2
  4.3 0.0 copy-start.3
  4.3 0.7 copy-done.3
  4.9 107.2 %shard_map.112 = (bf16[128,1024]{1,0:T(8,128)(2,1)S(1)}, bf16[128,1024]{1,0:T(8,128)(2,1)S(1)}, bf16[4,128,192]{2,1,0:T(8,128)(2,1)S(1)}) custom-call(s32[1,4]{1,0:T(1,128)S(1)} %copy-done.2, s32[1,4]{1,0:T(1,128)S(1)} %copy-done.3, bf16[128,1024]{1,0:T(8,128)(2,1)S(1)} %copy-done, bf16[128,1024]{1,0:T(8,128)(2,1)S(1)} %copy-done.1, ...), custom_call_target="tpu_custom_call" | custom-call | flops 7516192768 | bytes 16777216 | tf_op jit(solution)/shard_map/pallas_call | solution.py:462
  112.2 0.8 copy.13
  113.0 0.7 copy.16
  113.7 0.7 copy.17
Async XLA Ops:
  1.7 1.0 copy-start
  2.7 0.9 copy-start.1
  3.6 0.7 copy-start.2
  4.3 0.7 copy-start.3

commit v4 on v3

--- a/solution.py
+++ b/solution.py
@@ -30,19 +30,13 @@
 
 
 MESH = pl.DeviceIdType.MESH
-LANES = 128
+PARTS = 2
 
 
 def flip(i, k):
     if k % 2:
         i = i + 1 - 2 * (i % 2)
     return (i + 2) % 4 if k >= 2 else i
-
-
-def packed(block):
-    half = block.shape[0] // 2
-    rest = jnp.concatenate([block[:half, LANES:], block[half:, LANES:]], axis=1)
-    return jnp.concatenate([block[:, :LANES], rest], axis=0)
 
 
 def kernel(
@@ -103,10 +97,11 @@
     d, t = lax.axis_index("dp"), lax.axis_index("tensor")
     zz, gx = d // g, d % g
     tokens, width = hidden_hbm.shape
-    block_count, block_len, width_part = states_ref.shape
+    block_count, width_part, block_len = states_ref.shape
     rows_all = block_count * block_len
     pair_rows = CAP * block_len
     pairs = block_count // CAP
+    part = q_s.shape[1] // PARTS
     cols = w.shape[2]
     local = q_s.shape[1]
     head_size = local * tp // HEADS
@@ -148,14 +143,10 @@
     load_q, load_kv = [], []
     for k in range(tp):
         load_q.append(load(wq_hbm.at[pl.ds(flip(t, k) * width, width), :], wq.at[k]))
-    rest = width_part - LANES
     for k in range(tp):
         for hbm, here in ((kw_hbm, kw), (vw_hbm, vw)):
-            start = flip(t, k) * width_part
-            for first, size, to in ((0, LANES, k * LANES), (LANES, rest, tp * LANES + k * rest)):
-                load_kv.append(
-                    load(hbm.at[pl.ds(start + first, size), :], here.at[pl.ds(to, size), :])
-                )
+            rows = pl.ds(flip(t, k) * width_part, width_part)
+            load_kv.append(load(hbm.at[rows, :], here.at[pl.ds(k * width_part, width_part), :]))
 
     barrier = pltpu.get_barrier_semaphore()
     peers = [tensor_peer(1), tensor_peer(2), zz_peer(1), zz_peer(2)]
@@ -211,33 +202,40 @@
     def is_gap(gap, o):
         return jnp.where(gap == o, 1.0, 0.0).astype(F32)
 
+    turn_in = remote(grad_hbm, turned.at[0], turn_peer)
+    turn_local = pltpu.make_async_copy(grad_hbm, turned.at[0], local_sem.at[len(local_copies)])
+
+    @pl.when(jnp.logical_not(on_diagonal))
+    def _():
+        turn_in.start()
+
+    @pl.when(on_diagonal)
+    def _():
+        turn_local.start()
+
+    def send_weight(h):
+        rows = pl.ds(h * part, part)
+        return [
+            send(ow_hbm.at[rows, :], w.at[gx, rows, :], group_peer(k)) for k in range(1, g)
+        ]
+
+    weight_in = [send_weight(0)]
+    hidden_in = gather(hidden_hbm, hid, tensor_peer)
+    weight_in += [send_weight(h) for h in range(1, PARTS)]
+
     for copy in load_small:
         copy.wait()
     owner_gap = [(owner_ref[0, k * CAP] - d + dp_count) % dp_count for k in range(pairs)]
     target_gap = [(d - target_ref[0, k * CAP] + dp_count) % dp_count for k in range(pairs)]
-
-    pair_packs = [
-        packed(states_ref[pl.ds(k * CAP, CAP)].astype(F32).reshape(pair_rows, width_part))
-        for k in range(pairs)
-    ]
     blocks_in = []
     for o in range(1, WINDOW + 1):
-        block = sum(is_gap(target_gap[k], o) * pair_packs[k] for k in range(pairs))
-        out_blocks[o - 1] = block.astype(BF)
+        for i in range(CAP):
+            block = sum(
+                is_gap(target_gap[k], o) * states_ref[k * CAP + i].astype(F32)
+                for k in range(pairs)
+            )
+            out_blocks[o - 1, :, i * block_len : (i + 1) * block_len] = block.astype(BF)
         blocks_in.append(send(out_blocks.at[o - 1], arrived.at[o - 1], dp_peer(-o)))
-    turn_in = remote(grad_hbm, turned.at[0], turn_peer)
-    turn_local = pltpu.make_async_copy(grad_hbm, turned.at[0], local_sem.at[len(local_copies)])
-
-    @pl.when(jnp.logical_not(on_diagonal))
-    def _():
-        turn_in.start()
-
-    @pl.when(on_diagonal)
-    def _():
-        turn_local.start()
-
-    hidden_in = gather(hidden_hbm, hid, tensor_peer)
-    weight_in = [send(ow_hbm, w.at[gx], group_peer(k)) for k in range(1, g)]
 
     @pl.when(jnp.logical_not(on_diagonal))
     def _():
@@ -254,9 +252,8 @@
     for k in range(pairs):
         block = sum(
             is_gap(owner_gap[k], o) * arrived[o - 1].astype(F32) for o in range(1, WINDOW + 1)
-        ).astype(BF)
-        nbp[0, pl.ds(k * pair_rows, pair_rows), :] = block[:pair_rows]
-        nbp[0, pl.ds(rows_all + k * block_len, block_len), :] = block[pair_rows:]
+        )
+        nbp[0, :, k * pair_rows : (k + 1) * pair_rows] = block.astype(BF)
     nb_in = gather(nbp.at[0], nbp, tensor_peer)
 
     hidden_in.append(forwarded(hid, tensor_peer, hidden_in))
@@ -273,64 +270,66 @@
     nb_in.append(forwarded(nbp, tensor_peer, nb_in))
 
     load_w.wait()
-    for copy in weight_in:
-        copy.wait_recv()
     turned_in[0].wait_recv()
     turned_in[2].wait_recv()
 
-    def ga_partial(j):
+    def ga_partial(h, j):
         block = turned[flip(apart, j)]
-        ga_send[j] = sum(
-            dot_nt(block[:, m * cols : (m + 1) * cols], w[m]) for m in range(g)
+        ga_send[h, j] = sum(
+            dot_nt(block[:, m * cols : (m + 1) * cols], w[m, h * part : (h + 1) * part, :])
+            for m in range(g)
         ).astype(BF)
 
-    ga_partial(3)
-    ga_partial(1)
-    ga_in = scatter_start(ga_send, ga_recv, zz_peer)
-    ga_partial(2)
-    ga_partial(0)
+    def ga_start(h):
+        for copy in weight_in[h]:
+            copy.wait_recv()
+        ga_partial(h, 3)
+        ga_partial(h, 1)
+        copies = scatter_start(ga_send.at[h], ga_recv.at[h], zz_peer)
+        ga_partial(h, 2)
+        ga_partial(h, 0)
+        return copies
+
+    ga_in = [ga_start(0)]
 
     nb_in[0].wait_recv()
     nb_in[2].wait_recv()
-    for k in range(tp):
-        nb[:, k * LANES : (k + 1) * LANES] = nbp[k, pl.ds(0, rows_all), :]
-    for k in range(0, tp, 2):
-        for p in range(pairs):
-            rows = pl.ds(rows_all + p * block_len, block_len)
-            one, two = nbp[k, rows, :].astype(F32), nbp[k + 1, rows, :].astype(F32)
-            lanes = pl.ds(tp * LANES + k * rest, 2 * rest)
-            for half in range(2):
-                part = slice(half * rest, (half + 1) * rest)
-                joined = jnp.concatenate([one[:, part], two[:, part]], axis=1)
-                nb[pl.ds((p * CAP + half) * block_len, block_len), lanes] = joined.astype(BF)
+    for b in range(block_count):
+        block = nbp[:, :, b * block_len : (b + 1) * block_len]
+        nb[b * block_len : (b + 1) * block_len, :] = block.reshape(tp * width_part, block_len).T
     for copy in load_kv:
         copy.wait()
     for c in range(0, local, tile):
         at = pl.ds(c, tile)
         k_s[:, at] = dot(nb[...], kw[:, at]).astype(BF)
         v_s[:, at] = dot(nb[...], vw[:, at]).astype(BF)
-    scatter_middle(ga_send, ga_recv, zz_peer, ga_in)
-
-    heads = local // head_size
-
-    def forward(h, carry):
+    scatter_middle(ga_send.at[0], ga_recv.at[0], zz_peer, ga_in[0])
+    ga_in += [ga_start(h) for h in range(1, PARTS)]
+
+    heads = local // head_size // PARTS
+
+    def forward(first, n, carry):
+        h = first + n
         at = pl.ds(pl.multiple_of(h * head_size, head_size), head_size)
+        to = pl.ds(pl.multiple_of(n * head_size, head_size), head_size)
         for c in range(spans):
             mine, theirs = pl.ds(c * SPAN, SPAN), pl.ds(c * keys, keys)
             scores = dot_nt(q_s[mine, at], k_s[theirs, at]) * scale
             expanded = jnp.exp(scores - jnp.max(scores, axis=-1, keepdims=True))
             probs = expanded / jnp.sum(expanded, axis=-1, keepdims=True)
             probs_s[h, mine, :] = probs
-            att[0, mine, at] = dot(probs.astype(BF), v_s[theirs, at]).astype(BF)
+            att[first // heads, 0, mine, to] = dot(probs.astype(BF), v_s[theirs, at]).astype(BF)
         return carry
 
-    lax.fori_loop(0, heads, forward, 0, unroll=4)
-    att_in = gather(att.at[0], att, zz_peer)
-
-    ga_s[...] = scatter_end(ga_send, ga_recv, ga_in).astype(BF)
-    att_in.append(forwarded(att, zz_peer, att_in))
-
-    def backward(h, carry):
+    att_in = []
+    for h in range(PARTS):
+        lax.fori_loop(0, heads, functools.partial(forward, h * heads), 0, unroll=heads)
+        att_in.append(gather(att.at[h, 0], att.at[h], zz_peer))
+        if h:
+            scatter_middle(ga_send.at[h], ga_recv.at[h], zz_peer, ga_in[h])
+
+    def backward(first, n, carry):
+        h = first + n
         at = pl.ds(pl.multiple_of(h * head_size, head_size), head_size)
         for c in range(spans):
             mine, theirs = pl.ds(c * SPAN, SPAN), pl.ds(c * keys, keys)
@@ -342,33 +341,28 @@
             gv_s[theirs, at] = dot_tn(probs.astype(BF), ga).astype(BF)
         return carry
 
-    lax.fori_loop(0, heads, backward, 0, unroll=4)
-
-    for k in range(0, tp, 2):
-        at = pl.ds(k * LANES, 2 * LANES)
-        both = dot_nt(gk_s[...], kw[at, :]) + dot_nt(gv_s[...], vw[at, :])
-        for i in range(2):
-            st_send[k + i, pl.ds(0, rows_all), :] = both[:, i * LANES : (i + 1) * LANES].astype(BF)
-    at = pl.ds(tp * LANES, tp * rest)
-    both = dot_nt(gk_s[...], kw[at, :]) + dot_nt(gv_s[...], vw[at, :])
-    for k in range(tp):
-        part = slice(k * rest, (k + 1) * rest)
-        for p in range(pairs):
-            top = p * pair_rows
-            joined = jnp.concatenate(
-                [both[top : top + block_len, part], both[top + block_len : top + pair_rows, part]],
-                axis=1,
-            )
-            st_send[k, pl.ds(rows_all + p * block_len, block_len), :] = joined.astype(BF)
+    for h in range(PARTS):
+        total = scatter_end(ga_send.at[h], ga_recv.at[h], ga_in[h])
+        ga_s[:, h * part : (h + 1) * part] = total.astype(BF)
+        att_in[h].append(forwarded(att.at[h], zz_peer, att_in[h]))
+        lax.fori_loop(0, heads, functools.partial(backward, h * heads), 0, unroll=heads)
+
+    for c in range(0, rows_all, tile):
+        both = dot_nt(kw[...], gk_s[c : c + tile, :]) + dot_nt(vw[...], gv_s[c : c + tile, :])
+        for k in range(tp):
+            st_send[k, :, c : c + tile] = both[k * width_part : (k + 1) * width_part].astype(BF)
     st_in = scatter_start(st_send, st_recv, tensor_peer)
 
     def cross_partial(k):
-        block = att[flip(apart, k)]
+        slot = flip(apart, k)
         for m in range(g):
-            cp_send[k, :, m * cols : (m + 1) * cols] = dot(block, w[m]).astype(BF)
-
-    att_in[0].wait_recv()
-    att_in[2].wait_recv()
+            cp_send[k, :, m * cols : (m + 1) * cols] = sum(
+                dot(att[h, slot], w[m, h * part : (h + 1) * part, :]) for h in range(PARTS)
+            ).astype(BF)
+
+    for copies in att_in:
+        copies[0].wait_recv()
+        copies[2].wait_recv()
     cross_partial(3)
     cross_partial(1)
     cp_in = scatter_start(cp_send, cp_recv, tensor_peer)
@@ -387,12 +381,11 @@
     rows_s[...] = scatter_end(st_send, st_recv, st_in).astype(BF)
     ret_in = []
     for o in range(1, WINDOW + 1):
-        for first, size, to in ((0, pair_rows, 0), (rows_all, block_len, pair_rows)):
-            block = sum(
-                is_gap(owner_gap[k], o) * rows_s[pl.ds(first + k * size, size), :].astype(F32)
-                for k in range(pairs)
-            )
-            ret_send[o - 1, pl.ds(to, size), :] = block.astype(BF)
+        block = sum(
+            is_gap(owner_gap[k], o) * rows_s[:, k * pair_rows : (k + 1) * pair_rows].astype(F32)
+            for k in range(pairs)
+        )
+        ret_send[o - 1] = block.astype(BF)
         ret_in.append(send(ret_send.at[o - 1], ret_recv.at[o - 1], dp_peer(o)))
 
     co_mine[...] = scatter_end(cp_send, cp_recv, cp_in).astype(BF)
@@ -418,10 +411,7 @@
             is_gap(target_gap[k], o) * ret_recv[o - 1].astype(F32) for o in range(1, WINDOW + 1)
         )
         for i in range(CAP):
-            gst_ref[k * CAP + i, :, :LANES] = block[i * block_len : (i + 1) * block_len].astype(BF)
-            gst_ref[k * CAP + i, :, LANES:] = block[
-                pair_rows:, i * rest : (i + 1) * rest
-            ].astype(BF)
+            gst_ref[k * CAP + i] = block[:, i * block_len : (i + 1) * block_len].astype(BF)
 
     @pl.when(jnp.logical_not(on_diagonal))
     def _():
@@ -447,11 +437,13 @@
     g = dp_count // tp
     tokens, width = hidden.shape
     local = query_weight.shape[1]
-    block_count, block_len, width_part = neighbour_states.shape
+    states = jnp.swapaxes(neighbour_states, 1, 2)
+    block_count, width_part, block_len = states.shape
     rows = block_count * block_len
-    pack = rows * width_part // LANES
+    pair_rows = CAP * block_len
+    part = local // PARTS
     heads = HEADS // tp
-    copies = 2 * WINDOW + 8 * (tp - 1) + (g - 1) + 2
+    copies = 2 * WINDOW + (6 + 2 * PARTS) * (tp - 1) + PARTS * (g - 1) + 2
 
     def vmem(*shape, kind=BF):
         return pltpu.VMEM(shape, kind)
@@ -459,45 +451,45 @@
     in_vmem = pl.BlockSpec(memory_space=pltpu.VMEM)
     anywhere = pl.BlockSpec(memory_space=pl.ANY)
     multiply_adds = tokens * tp * width * local * 4 + rows * local * tp * width_part * 4
-    return pl.pallas_call(
+    cross, grad_hidden, grad_states = pl.pallas_call(
         functools.partial(kernel, dp_count, tp),
         in_specs=[anywhere] * 9,
         out_specs=[in_vmem] * 3,
         out_shape=[
             jax.ShapeDtypeStruct(hidden.shape, BF),
             jax.ShapeDtypeStruct(hidden.shape, BF),
-            jax.ShapeDtypeStruct(neighbour_states.shape, BF),
+            jax.ShapeDtypeStruct(states.shape, BF),
         ],
         scratch_shapes=[
             pltpu.SMEM(block_owner.shape, jnp.int32),
             pltpu.SMEM(slot_target.shape, jnp.int32),
-            vmem(*neighbour_states.shape),
+            vmem(*states.shape),
             vmem(tp, width, local),
             vmem(tp * width_part, local),
             vmem(tp * width_part, local),
             vmem(g, *out_weight.shape),
             vmem(tp, tokens, width),
             vmem(tp, tokens, width),
-            vmem(tp, tokens, local),
-            vmem(tp, tokens, local),
-            vmem(WINDOW, 3 * block_len, LANES),
-            vmem(WINDOW, 3 * block_len, LANES),
-            vmem(tp, pack, LANES),
+            vmem(PARTS, tp, tokens, part),
+            vmem(PARTS, tp, tokens, part),
+            vmem(WINDOW, width_part, pair_rows),
+            vmem(WINDOW, width_part, pair_rows),
+            vmem(tp, width_part, rows),
             vmem(rows, tp * width_part),
             vmem(tokens, local),
             vmem(rows, local),
             vmem(rows, local),
-            vmem(tp, tokens, local),
+            vmem(PARTS, tp, tokens, part),
             vmem(heads, tokens, K_NB * block_len, kind=F32),
             vmem(tokens, local),
             vmem(tokens, local),
             vmem(rows, local),
             vmem(rows, local),
-            vmem(tp, pack, LANES),
-            vmem(tp, pack, LANES),
-            vmem(pack, LANES),
-            vmem(WINDOW, 3 * block_len, LANES),
-            vmem(WINDOW, 3 * block_len, LANES),
+            vmem(tp, width_part, rows),
+            vmem(tp, width_part, rows),
+            vmem(width_part, rows),
+            vmem(WINDOW, width_part, pair_rows),
+            vmem(WINDOW, width_part, pair_rows),
             vmem(tp, tokens, width),
             vmem(tp, tokens, width),
             vmem(tp, tokens, width),
@@ -506,25 +498,26 @@
             vmem(tokens, width),
             pltpu.SemaphoreType.DMA((copies,)),
             pltpu.SemaphoreType.DMA((copies,)),
-            pltpu.SemaphoreType.DMA((5 * tp + 6,)),
+            pltpu.SemaphoreType.DMA((3 * tp + 6,)),
         ],
         cost_estimate=pl.CostEstimate(
             flops=2 * multiply_adds, bytes_accessed=16 * 2**20, transcendentals=0
         ),
         compiler_params=pltpu.CompilerParams(
-            collective_id=0, has_side_effects=True, vmem_limit_bytes=52 * 2**20
+            collective_id=0, has_side_effects=True, vmem_limit_bytes=60 * 2**20
         ),
     )(
         block_owner,
         slot_target,
         hidden,
         grad_out,
-        neighbour_states,
+        states,
         query_weight,
         key_weight,
         value_weight,
         out_weight,
     )
+    return cross, grad_hidden, jnp.swapaxes(grad_states, 1, 2)
 
 
 def solution(mesh):

time: 115 us -> 110 us (0.957)
  Pallas kernels: 107 us -> 104 us
  local copies, waits for them, and re-layouts: 6.49 us -> 4.95 us
    pallas_call x1, Pallas kernels: 107 us -> 104 us  [shards(): pl.pallas_call(functools.partial(kernel, dp_count, tp), in_specs=[anywher...]
    unnamed x11 -> x3, local copies, waits for them, and re-layouts: 5.67 us -> 4.95 us
where the time goes in v4:
time: 110 us
  Pallas kernels  104 us (95%)
  local copies, waits for them, and re-layouts  4.95 us (4%)
    pallas_call x1, Pallas kernels, shards(): pl.pallas_call(functools.partial(kernel, dp_count, tp), in_specs=[anywher...  104 us
    unnamed x3, local copies, waits for them, and re-layouts  4.95 us

profile of v4, /device:TPU:4, one launch (start us, length us, event | category | flops | bytes accessed | tf_op | source)
XLA Modules:
  0.0 109.6 jit_solution(3311667220615404486)
XLA Ops:
  0.6 104.0 %shard_map.112 = (bf16[128,1024]{1,0:T(8,128)(2,1)}, bf16[128,1024]{1,0:T(8,128)(2,1)}, bf16[4,192,128]{2,1,0:T(8,128)(2,1)}) custom-call(s32[1,4]{1,0:T(1,128)} %owner_hbm.1, s32[1,4]{1,0:T(1,128)} %target_hbm.1, bf16[128,1024]{1,0:T(8,128)(2,1)} %hidden_hbm.1, bf16[128,1024]{1,0:T(8,128)(2,1)} %grad_hbm.1, bf16[4,192,128]{2,1,0:T(8,128)(2,1)} %bitcast.3, ...), custom_call_target="tpu_custom_call" | custom-call | flops 7516192768 | bytes 16777216 | tf_op jit(solution)/shard_map/pallas_call | solution.py:454
  104.7 1.7 %copy.15 = bf16[128,1024]{1,0:T(8,128)(2,1)} copy(bf16[128,1024]{1,0:T(8,128)(2,1)} %get-tuple-element.12) | data formatting | bytes 524288
  106.4 1.7 %copy.16 = bf16[128,1024]{1,0:T(8,128)(2,1)} copy(bf16[128,1024]{1,0:T(8,128)(2,1)} %get-tuple-element.13) | data formatting | bytes 524288
  108.0 1.6 %copy.17 = bf16[4,128,192]{1,2,0:T(8,128)(2,1)} copy(bf16[4,128,192]{1,2,0:T(8,128)(2,1)} %bitcast.2) | data formatting | bytes 393216

commit v5 on v4

--- a/solution.py
+++ b/solution.py
@@ -353,30 +353,51 @@
             st_send[k, :, c : c + tile] = both[k * width_part : (k + 1) * width_part].astype(BF)
     st_in = scatter_start(st_send, st_recv, tensor_peer)
 
-    def cross_partial(k):
+    def hidden_partial(k):
+        hp_send[k] = dot_nt(gq_s[...], wq[k]).astype(BF)
+
+    hidden_partial(3)
+    hidden_partial(1)
+    hp_in = scatter_start(hp_send, hp_recv, tensor_peer)
+    scatter_middle(st_send, st_recv, tensor_peer, st_in)
+
+    share = g // PARTS
+
+    def cross_partial(c, k):
         slot = flip(apart, k)
-        for m in range(g):
-            cp_send[k, :, m * cols : (m + 1) * cols] = sum(
-                dot(att[h, slot], w[m, h * part : (h + 1) * part, :]) for h in range(PARTS)
+        for i in range(share):
+            cp_send[c, k, :, i * cols : (i + 1) * cols] = sum(
+                dot(att[h, slot], w[c * share + i, h * part : (h + 1) * part, :])
+                for h in range(PARTS)
             ).astype(BF)
+
+    def cross_start(c):
+        cross_partial(c, 3)
+        cross_partial(c, 1)
+        copies = scatter_start(cp_send.at[c], cp_recv.at[c], tensor_peer)
+        cross_partial(c, 2)
+        scatter_middle(cp_send.at[c], cp_recv.at[c], tensor_peer, copies)
+        cross_partial(c, 0)
+        return copies
+
+    def cross_turn(c):
+        co_mine[c] = scatter_end(cp_send.at[c], cp_recv.at[c], cp_in[c]).astype(BF)
+        copy = remote(co_mine.at[c], co_last.at[c], turn_peer)
+
+        @pl.when(jnp.logical_not(on_diagonal))
+        def _():
+            copy.start()
+
+        @pl.when(on_diagonal)
+        def _():
+            co_last[c] = co_mine[c]
+
+        return copy
 
     for copies in att_in:
         copies[0].wait_recv()
         copies[2].wait_recv()
-    cross_partial(3)
-    cross_partial(1)
-    cp_in = scatter_start(cp_send, cp_recv, tensor_peer)
-    scatter_middle(st_send, st_recv, tensor_peer, st_in)
-    cross_partial(2)
-    scatter_middle(cp_send, cp_recv, tensor_peer, cp_in)
-    cross_partial(0)
-
-    def hidden_partial(k):
-        hp_send[k] = dot_nt(gq_s[...], wq[k]).astype(BF)
-
-    hidden_partial(3)
-    hidden_partial(1)
-    hp_in = scatter_start(hp_send, hp_recv, tensor_peer)
+    cp_in = [cross_start(0)]
 
     rows_s[...] = scatter_end(st_send, st_recv, st_in).astype(BF)
     ret_in = []
@@ -387,20 +408,11 @@
         )
         ret_send[o - 1] = block.astype(BF)
         ret_in.append(send(ret_send.at[o - 1], ret_recv.at[o - 1], dp_peer(o)))
-
-    co_mine[...] = scatter_end(cp_send, cp_recv, cp_in).astype(BF)
-    cross_in = remote(co_mine, co_last, turn_peer)
-
-    @pl.when(jnp.logical_not(on_diagonal))
-    def _():
-        cross_in.start()
-
-    @pl.when(on_diagonal)
-    def _():
-        co_last[...] = co_mine[...]
-
+    cp_in += [cross_start(c) for c in range(1, PARTS)]
+    cross_in = [cross_turn(0)]
     hidden_partial(2)
     scatter_middle(hp_send, hp_recv, tensor_peer, hp_in)
+    cross_in += [cross_turn(c) for c in range(1, PARTS)]
     hidden_partial(0)
     gh_ref[...] = scatter_end(hp_send, hp_recv, hp_in).astype(BF)
 
@@ -415,9 +427,11 @@
 
     @pl.when(jnp.logical_not(on_diagonal))
     def _():
-        cross_in.wait()
-
-    cross_ref[...] = co_last[...]
+        for copy in cross_in:
+            copy.wait()
+
+    for c in range(PARTS):
+        cross_ref[:, c * share * cols : (c + 1) * share * cols] = co_last[c]
     for copy in sent:
         copy.wait_send()
 
@@ -443,7 +457,7 @@
     pair_rows = CAP * block_len
     part = local // PARTS
     heads = HEADS // tp
-    copies = 2 * WINDOW + (6 + 2 * PARTS) * (tp - 1) + PARTS * (g - 1) + 2
+    copies = 2 * WINDOW + (5 + 3 * PARTS) * (tp - 1) + PARTS * (g - 1) + 1 + PARTS
 
     def vmem(*shape, kind=BF):
         return pltpu.VMEM(shape, kind)
@@ -492,10 +506,10 @@
             vmem(WINDOW, width_part, pair_rows),
             vmem(tp, tokens, width),
             vmem(tp, tokens, width),
-            vmem(tp, tokens, width),
-            vmem(tp, tokens, width),
-            vmem(tokens, width),
-            vmem(tokens, width),
+            vmem(PARTS, tp, tokens, width // PARTS),
+            vmem(PARTS, tp, tokens, width // PARTS),
+            vmem(PARTS, tokens, width // PARTS),
+            vmem(PARTS, tokens, width // PARTS),
             pltpu.SemaphoreType.DMA((copies,)),
             pltpu.SemaphoreType.DMA((copies,)),
             pltpu.SemaphoreType.DMA((3 * tp + 6,)),
@@ -504,7 +518,7 @@
             flops=2 * multiply_adds, bytes_accessed=16 * 2**20, transcendentals=0
         ),
         compiler_params=pltpu.CompilerParams(
-            collective_id=0, has_side_effects=True, vmem_limit_bytes=60 * 2**20
+            collective_id=0, has_side_effects=True, vmem_limit_bytes=58 * 2**20
         ),
     )(
         block_owner,

time: 110 us -> 109 us (level); the launches traced: 110 us -> 107 us
  Pallas kernels: 104 us -> 102 us
    pallas_call x1, Pallas kernels: 104 us -> 102 us  [shards(): pl.pallas_call(functools.partial(kernel, dp_count, tp), in_specs=[anywher...]
where the time goes in v5:
time: 109 us; the launch traced here: 107 us
  Pallas kernels  102 us (94%)
  local copies, waits for them, and re-layouts  4.95 us (5%)
    pallas_call x1, Pallas kernels, shards(): pl.pallas_call(functools.partial(kernel, dp_count, tp), in_specs=[anywher...  102 us
    unnamed x3, local copies, waits for them, and re-layouts  4.95 us

profile of v5, /device:TPU:4, one launch (start us, length us, event | category | flops | bytes accessed | tf_op | source)
XLA Modules:
  0.0 107.4 jit_solution(2341284676425072207)
XLA Ops:
  0.6 101.9 %shard_map.112 = (bf16[128,1024]{1,0:T(8,128)(2,1)}, bf16[128,1024]{1,0:T(8,128)(2,1)}, bf16[4,192,128]{2,1,0:T(8,128)(2,1)}) custom-call(s32[1,4]{1,0:T(1,128)} %owner_hbm.1, s32[1,4]{1,0:T(1,128)} %target_hbm.1, bf16[128,1024]{1,0:T(8,128)(2,1)} %hidden_hbm.1, bf16[128,1024]{1,0:T(8,128)(2,1)} %grad_hbm.1, bf16[4,192,128]{2,1,0:T(8,128)(2,1)} %bitcast.3, ...), custom_call_target="tpu_custom_call" | custom-call | flops 7516192768 | bytes 16777216 | tf_op jit(solution)/shard_map/pallas_call | solution.py:468
  102.5 1.7 %copy.15 = bf16[128,1024]{1,0:T(8,128)(2,1)} copy(bf16[128,1024]{1,0:T(8,128)(2,1)} %get-tuple-element.12) | data formatting | bytes 524288
  104.2 1.7 %copy.16 = bf16[128,1024]{1,0:T(8,128)(2,1)} copy(bf16[128,1024]{1,0:T(8,128)(2,1)} %get-tuple-element.13) | data formatting | bytes 524288
  105.8 1.6 %copy.17 = bf16[4,128,192]{1,2,0:T(8,128)(2,1)} copy(bf16[4,128,192]{1,2,0:T(8,128)(2,1)} %bitcast.2) | data formatting | bytes 393216
